TPU v7x, 32 devices: a whole 2x2x4 slice. The times are simulated.
32 devices in a mesh: dp: 4 (over y, x), seq: 8 (over z, core).
Axes of the slice: x: 2, y: 2, z: 4, core: 2. Of those that a mesh axis runs over, the one named last changes fastest.
Arguments:
- tokens: bfloat16 [10240, 2048], P(('dp', 'seq')), may hold values from -6 to 6
- lengths: int32 [4, 2], P('dp'), may hold values from 1 to 2048, 2560 in all within a row
- attention_gain: bfloat16 [2048], P('seq'), may hold values from 0.5 to 1.5
- query_weight: bfloat16 [2048, 2048], P('seq'), may hold values from -0.1875 to 0.1875
- key_weight: bfloat16 [2048, 256], P('seq'), may hold values from -0.1875 to 0.1875
- value_weight: bfloat16 [2048, 256], P('seq'), may hold values from -0.125 to 0.125
- output_weight: bfloat16 [2048, 2048], P('seq'), may hold values from -0.375 to 0.375
- feedforward_gain: bfloat16 [2048], P('seq'), may hold values from 0.5 to 1.5
- gate_weight: bfloat16 [2048, 5632], P('seq'), may hold values from -0.125 to 0.125
- up_weight: bfloat16 [2048, 5632], P('seq'), may hold values from -0.125 to 0.125
- down_weight: bfloat16 [5632, 2048], P('seq'), may hold values from -0.078125 to 0.078125
- cotangent: bfloat16 [10240, 2048], P(('dp', 'seq')), may hold values from -6 to 6
Outputs:
- layer_output: bfloat16 [10240, 2048], P(('dp', 'seq'))
- token_gradient: float32 [10240, 2048], P(('dp', 'seq'))
- attention_gain_gradient: float32 [2048], P('seq')
- query_gradient: float32 [2048, 2048], P('seq')
- key_gradient: float32 [2048, 256], P('seq')
- value_gradient: float32 [2048, 256], P('seq')
- output_gradient: float32 [2048, 2048], P('seq')
- feedforward_gain_gradient: float32 [2048], P('seq')
- gate_gradient: float32 [2048, 5632], P('seq')
- up_gradient: float32 [2048, 5632], P('seq')
- down_gradient: float32 [5632, 2048], P('seq')
Inputs may be any that keep to these rules, and one draw needn't show every extreme that they name: Each row lists the lengths of the 2 sequences packed in order into one data group's 2560 tokens; a row sums to 2560 and its longest length is at most 2048.
All inputs are finite; a program needn't handle non-finite values.
Results may differ from a plain program's by a relative error of at most 0.022.
Values may be sent and summed in bfloat16 or wider, within the bound.
No kernel may reach another device: no remote copies, remote signals or barrier semaphores. Data moves between devices by JAX's collectives and lax.ppermute only.
A program may use at most 384 MiB of HBM per device.

v0:
```python
import functools

import jax
import jax.numpy as jnp
from jax import lax
from jax.experimental import pallas as pl
from jax.experimental.pallas import tpu as pltpu
from jax.sharding import PartitionSpec as P

HEADS = 32
HEAD_DIM = 64
KV_HEADS = 4
EPS = 1e-05
ROPE_BASE = 10000.0
NEG = -1e30
TILE_FORTH = 2560
TILE_BACK = 2560
VMEM_LIMIT = 56 * 2**20
BF = jnp.bfloat16
F32 = jnp.float32

NT = (((1,), (1,)), ((), ()))
TN = (((0,), (0,)), ((), ()))
NN = (((1,), (0,)), ((), ()))


def dot(left, right, dims=NN):
    return lax.dot_general(left, right, dims, preferred_element_type=F32)


def params(*semantics):
    return pltpu.CompilerParams(
        dimension_semantics=semantics, vmem_limit_bytes=VMEM_LIMIT
    )


FREE = pl.CostEstimate(flops=1, bytes_accessed=1, transcendentals=0)
TIMES = {
    "project": 0.1,
    "attend": 400,
    "attend_back": 1000,
    "merge": 1,
    "output_product": 3,
    "hidden_back": 4,
    "gate_product": 2,
    "up_gradient": 2,
    "up_product": 100,
    "back_product": 4,
    "back_first": 4,
    "down_gradient": 0.2,
    "gate_gradient": 2,
    "middle_back": 200,
    "down_product": 4,
    "output_gradient": 2,
    "project_back": 2,
    "sum_output": 100,
    "sum_tokens": 100,
    "spread_up": 300,
    "spread_gate": 0.1,
    "pick_columns": 2,
    "finish": 3,
}


def cost(name):
    time = TIMES[name]
    return pl.CostEstimate(
        flops=int(time * 8e8), bytes_accessed=int(time * 2.5e6), transcendentals=0
    )
ANYWHERE = pl.BlockSpec(memory_space=pl.ANY)
SCALARS = pl.BlockSpec(memory_space=pltpu.SMEM)
INSIDE = pl.BlockSpec(memory_space=pltpu.VMEM)


def array(shape, dtype=BF):
    return jax.ShapeDtypeStruct(tuple(shape), dtype)


def tie(value, *others):
    return pl.pallas_call(
        lambda *refs: None,
        out_shape=array(value.shape, value.dtype),
        in_specs=[ANYWHERE] * (1 + len(others)),
        out_specs=ANYWHERE,
        input_output_aliases={0: 0},
        cost_estimate=FREE,
        name="tie",
    )(value, *others)


def run(body, name, grid, ins, outs, needs=(), scratch=(), aliases=None):
    count, made = len(ins), len(outs)

    def kernel(*refs):
        body(refs[:count], refs[count + len(needs) :][:made], refs[count + len(needs) + made :])

    result = pl.pallas_call(
        kernel,
        grid=grid,
        out_shape=tuple(shape for shape, _ in outs),
        in_specs=[spec for _, spec in ins] + [ANYWHERE] * len(needs),
        out_specs=tuple(spec for _, spec in outs),
        scratch_shapes=list(scratch),
        input_output_aliases=aliases or {},
        compiler_params=params(*["arbitrary"] * len(grid)),
        cost_estimate=cost(name),
        name=name,
    )(*[value for value, _ in ins], *needs)
    return result


def whole(shape):
    return pl.BlockSpec(tuple(shape), lambda i: (0,) * len(shape), pipeline_mode=pl.Buffered(1))


def down_rows(rows, cols, at=None):
    return pl.BlockSpec((rows, cols), (lambda i: (i, 0)) if at is None else (lambda i: (at, 0)))


def along_cols(rows, cols, at=0):
    return pl.BlockSpec((rows, cols), lambda i: (at, i))


def pick_kernel(which, gain, gate, up, gate_out, up_out, *, shards):
    piece = gate.shape[1] // (4 * shards)
    scale = gain[...]
    for quarter in range(4):

        @pl.when(which[0] == quarter)
        def _():
            for source, out in ((gate, gate_out), (up, up_out)):
                whole = source[...].astype(F32) * scale
                parts = []
                for shard in range(shards):
                    first = (shard * 4 + quarter) * piece
                    parts.append(whole[:, first : first + piece])
                out[...] = jnp.concatenate(parts, axis=1).astype(BF)


def pick_columns(quarter, gain, gate, up, shards):
    rows, width = gate.shape
    vmem = pl.BlockSpec(memory_space=pltpu.VMEM)
    shape = jax.ShapeDtypeStruct((rows, width // 4), BF)
    return pl.pallas_call(
        functools.partial(pick_kernel, shards=shards),
        out_shape=(shape, shape),
        in_specs=[pl.BlockSpec(memory_space=pltpu.SMEM), vmem, vmem, vmem],
        out_specs=(vmem, vmem),
        compiler_params=params(),
        cost_estimate=cost("pick_columns"),
        name="pick_columns",
    )(quarter, gain, gate, up)


def spread_kernel(which, grads, gain, weight, out, gain_out, *, shards):
    piece = grads.shape[2] // shards
    chunks = [grads[which[0] ^ quarter].astype(F32) for quarter in range(4)]
    whole = jnp.concatenate(
        [
            chunks[quarter][:, shard * piece : (shard + 1) * piece]
            for shard in range(shards)
            for quarter in range(4)
        ],
        axis=1,
    )
    gain_out[...] = jnp.sum(whole * weight[...].astype(F32), axis=1, keepdims=True)
    out[...] = whole * gain[...]


def spread_columns(name, mine, grads, gain, weight, shards):
    rows, width = weight.shape
    block = min(rows, 64)
    row = lambda cols: pl.BlockSpec((block, cols), lambda i: (i, 0))
    return pl.pallas_call(
        functools.partial(spread_kernel, shards=shards),
        grid=(rows // block,),
        out_shape=(
            jax.ShapeDtypeStruct((rows, width), F32),
            jax.ShapeDtypeStruct((rows, 1), F32),
        ),
        in_specs=[
            pl.BlockSpec(memory_space=pltpu.SMEM),
            pl.BlockSpec((4, block, width // 4), lambda i: (0, i, 0)),
            row(1),
            row(width),
        ],
        out_specs=(row(width), row(1)),
        compiler_params=params("arbitrary"),
        cost_estimate=cost(name),
        name=name,
    )(mine, grads, gain, weight)


def turn(values, cos_t, sin_t):
    lane = lax.broadcasted_iota(jnp.int32, values.shape, 1)
    other = jnp.where(
        lane % 64 < 32, pltpu.roll(values, 96, 1), pltpu.roll(values, 32, 1)
    )
    return values * cos_t + other * sin_t


def project_kernel(ins, outs, _):
    *xs, w_ref, cos_ref, sin_ref = ins
    hat_ref, q_ref, kv_ref = outs
    rows = hat_ref.shape[0] // len(xs)
    for i, x_ref in enumerate(xs):
        span = slice(i * rows, (i + 1) * rows)
        x = x_ref[...].astype(F32)
        scale = lax.rsqrt(jnp.mean(x * x, axis=1, keepdims=True) + EPS)
        hat_ref[span, :] = (x * scale).astype(BF)
    out = dot(hat_ref[...], w_ref[...])
    cos_t, sin_t = cos_ref[...], sin_ref[...]
    wide = q_ref.shape[1]
    for pair in range(wide // 128):
        part = turn(out[:, pair * 128 : pair * 128 + 128], cos_t, sin_t)
        q_ref[:, pair * 128 : pair * 128 + 128] = (part * HEAD_DIM**-0.5).astype(BF)
    kv = out[:, wide : wide + 128]
    lane = lax.broadcasted_iota(jnp.int32, kv.shape, 1)
    kv_ref[...] = jnp.where(lane < 64, turn(kv, cos_t, sin_t), kv).astype(BF)


def project(chunk, xs, weight, cos_t, sin_t, rows, before=()):
    depth, wide = weight.shape[0], weight.shape[1] - 128
    ins = [(x, whole(x.shape)) for x in xs] + [
        (weight, whole(weight.shape)),
        (cos_t, down_rows(rows, 128, chunk)),
        (sin_t, down_rows(rows, 128, chunk)),
    ]

    def body(refs, outs, scratch):
        project_kernel(refs[: len(xs) + 3], outs, scratch)

    first = len(ins)
    return run(
        body,
        "project",
        (1,),
        ins + [(b, ANYWHERE) for b in before],
        [
            (array((4 * rows, cols)), down_rows(rows, cols, chunk))
            for cols in (depth, wide, 128)
        ],
        aliases={first + i: i for i in range(len(before))},
    )


def stack_heads(source, target, rows, upper):
    lane = lax.broadcasted_iota(jnp.int32, (rows, 128), 1)
    keep = (lane >= 64) if upper else (lane < 64)
    for head in range(source.shape[1] // 64):
        slab = source[:, head // 2 * 128 : head // 2 * 128 + 128].astype(F32)
        if (head % 2 == 1) != upper:
            slab = pltpu.roll(slab, 64, 1)
        target[head * rows : head * rows + rows, :] = jnp.where(keep, slab, 0.0).astype(BF)


def allowed(bounds, chunk, rows):
    low = bounds[0:1, :] - chunk * rows
    high = bounds[1:2, :] - chunk * rows
    place = lax.broadcasted_iota(jnp.int32, (rows, bounds.shape[1]), 0)
    return (place >= low) & (place <= high)


def over_chunks(where, step):
    group = pl.program_id(0)
    first, split, last = where[group], where[4 + group], where[8]
    edge = split - first

    def edges(i, carry):
        step(jnp.where(i < edge, first + i, last), True)
        return carry

    def inner(chunk, carry):
        step(chunk, False)
        return carry

    lax.fori_loop(split, last, inner, 0)
    lax.fori_loop(0, edge + 1, edges, 0)


def tiles_of(width, tile):
    return [slice(i, i + tile) for i in range(0, width, tile)]


def attend_kernel(where, q_ref, kv_ref, bound_ref, *rest, rows):
    out_ref, lse_ref, stacked, tops, totals, accs = rest[-6:]
    pairs = q_ref.shape[1] // 128
    stack_heads(q_ref, stacked, rows, False)
    lane = lax.broadcasted_iota(jnp.int32, (rows, 128), 1)
    tops[...] = jnp.full(tops.shape, NEG, F32)
    totals[...] = jnp.zeros(totals.shape, F32)
    accs[...] = jnp.zeros(accs.shape, F32)

    def step(chunk, masked):
        kv = kv_ref[chunk]
        for tile in tiles_of(2 * pairs * rows, TILE_FORTH):
            scores = dot(kv, stacked[tile, :], NT)
            if masked:
                mask = allowed(bound_ref[0, :, tile], chunk, rows)
                scores = jnp.where(mask, scores, NEG)
            top = tops[:, tile]
            peak = jnp.maximum(top, jnp.max(scores, axis=0, keepdims=True))
            fade = jnp.exp(top - peak)
            weights = jnp.exp(scores - peak)
            tops[:, tile] = peak
            totals[:, tile] = totals[:, tile] * fade + jnp.sum(
                weights, axis=0, keepdims=True
            )
            accs[:, tile] = accs[:, tile] * fade + dot(kv, weights.astype(BF), TN)[64:128]

    over_chunks(where, step)
    lse_ref[0] = tops[...] + jnp.log(totals[...])
    for pair in range(pairs):
        both = slice(pair * 2 * rows, (pair + 1) * 2 * rows)
        half = accs[:, both] / totals[:, both]
        flat = jnp.concatenate([half, half], axis=0).T
        out_ref[:, pair * 128 : pair * 128 + 128] = jnp.where(
            lane < 64, flat[:rows], flat[rows:]
        ).astype(BF)


def attend(where, queries, kv, bounds, rows, needs=()):
    shards = kv.shape[0]
    wide = queries.shape[1]
    lanes = wide // 64 * rows
    return pl.pallas_call(
        functools.partial(attend_kernel, rows=rows),
        grid_spec=pltpu.PrefetchScalarGridSpec(
            num_scalar_prefetch=1,
            grid=(4,),
            in_specs=[
                pl.BlockSpec((rows, wide), lambda g, w: (g, 0)),
                pl.BlockSpec((shards, rows, 128), lambda g, w: (0, g, 0)),
                pl.BlockSpec((1, 2, lanes), lambda g, w: (g, 0, 0)),
                *[ANYWHERE] * len(needs),
            ],
            out_specs=(
                pl.BlockSpec((rows, wide), lambda g, w: (g, 0)),
                pl.BlockSpec((1, 1, lanes), lambda g, w: (g, 0, 0)),
            ),
            scratch_shapes=[
                pltpu.VMEM((lanes, 128), BF),
                pltpu.VMEM((1, lanes), F32),
                pltpu.VMEM((1, lanes), F32),
                pltpu.VMEM((64, lanes), F32),
            ],
        ),
        out_shape=(
            jax.ShapeDtypeStruct((4 * rows, wide), BF),
            jax.ShapeDtypeStruct((4, 1, lanes), F32),
        ),
        compiler_params=params("arbitrary"),
        cost_estimate=cost("attend"),
        name="attend",
    )(where, queries, kv, bounds, *needs)


def attend_back_kernel(
    where,
    q_ref,
    kv_ref,
    bound_ref,
    up_ref,
    out_ref,
    lse_ref,
    cos_ref,
    sin_ref,
    *rest,
    rows,
):
    dq_ref, dkv_ref, stacked, upward, dq_acc, deltas = rest[-6:]
    group = pl.program_id(0)
    first, last = where[group], where[8]
    shards = kv_ref.shape[0]
    pairs = q_ref.shape[1] // 128
    stack_heads(q_ref, stacked, rows, False)
    stack_heads(up_ref, upward, rows, True)
    lane = lax.broadcasted_iota(jnp.int32, (rows, 128), 1)
    for pair in range(pairs):
        slab = up_ref[:, pair * 128 : pair * 128 + 128].astype(F32)
        slab = slab * out_ref[:, pair * 128 : pair * 128 + 128].astype(F32)
        both = jnp.concatenate(
            [jnp.where(lane < 64, slab, 0.0), jnp.where(lane < 64, 0.0, slab)], axis=0
        )
        deltas[:, pair * 2 * rows : (pair + 1) * 2 * rows] = jnp.sum(
            both.T, axis=0, keepdims=True
        )
    dq_acc[...] = jnp.zeros(dq_acc.shape, F32)

    def clear(chunk, carry):
        dkv_ref[chunk] = jnp.zeros((rows, 128), BF)
        return carry

    lax.fori_loop(0, first, clear, 0)
    lax.fori_loop(last + 1, shards, clear, 0)

    def step(chunk, masked):
        kv = kv_ref[chunk]
        total = jnp.zeros((rows, 128), F32)
        for tile in tiles_of(2 * pairs * rows, TILE_BACK):
            queries = stacked[tile, :]
            ups = upward[tile, :]
            weights = jnp.exp(dot(kv, queries, NT) - lse_ref[0, :, tile])
            if masked:
                mask = allowed(bound_ref[0, :, tile], chunk, rows)
                weights = jnp.where(mask, weights, 0.0)
            d_scores = (weights * (dot(kv, ups, NT) - deltas[:, tile])).astype(BF)
            total = total + dot(d_scores, queries) + dot(weights.astype(BF), ups)
            dq_acc[:, tile] += dot(kv, d_scores, TN)[0:64]
        dkv_ref[chunk] = total.astype(BF)

    over_chunks(where, step)
    cos_t, sin_t = cos_ref[...], sin_ref[...]
    for pair in range(pairs):
        half = dq_acc[:, pair * 2 * rows : (pair + 1) * 2 * rows]
        flat = jnp.concatenate([half, half], axis=0).T
        slab = jnp.where(lane < 64, flat[:rows], flat[rows:])
        dq_ref[:, pair * 128 : pair * 128 + 128] = turn(
            slab * HEAD_DIM**-0.5, cos_t, -sin_t
        ).astype(BF)


def attend_back(
    where, queries, kv, bounds, upstream, out, lse, cos_t, sin_t, rows, needs=()
):
    shards = kv.shape[0]
    wide = queries.shape[1]
    lanes = wide // 64 * rows
    row = lambda cols: pl.BlockSpec((rows, cols), lambda g, w: (g, 0))
    every = pl.BlockSpec((shards, rows, 128), lambda g, w: (0, g, 0))
    line = lambda count: pl.BlockSpec((1, count, lanes), lambda g, w: (g, 0, 0))
    return pl.pallas_call(
        functools.partial(attend_back_kernel, rows=rows),
        grid_spec=pltpu.PrefetchScalarGridSpec(
            num_scalar_prefetch=1,
            grid=(4,),
            in_specs=[
                row(wide),
                every,
                line(2),
                row(wide),
                row(wide),
                line(1),
                row(128),
                row(128),
                *[ANYWHERE] * len(needs),
            ],
            out_specs=(row(wide), every),
            scratch_shapes=[
                pltpu.VMEM((lanes, 128), BF),
                pltpu.VMEM((lanes, 128), BF),
                pltpu.VMEM((64, lanes), F32),
                pltpu.VMEM((1, lanes), F32),
            ],
        ),
        out_shape=(
            jax.ShapeDtypeStruct((4 * rows, wide), BF),
            jax.ShapeDtypeStruct(kv.shape, BF),
        ),
        compiler_params=params("arbitrary"),
        cost_estimate=cost("attend_back"),
        name="attend_back",
    )(where, queries, kv, bounds, upstream, out, lse, cos_t, sin_t, *needs)


def row_product(name, left, right, dims, block, needs=()):
    total = left.shape[1] if dims is TN else left.shape[0]
    cols = right.shape[0] if dims is NT else right.shape[1]
    spec = (
        along_cols(left.shape[0], block) if dims is TN else down_rows(block, left.shape[1])
    )

    def body(ins, outs, _):
        outs[0][...] = dot(ins[0][...], ins[1][...], dims).astype(BF)

    return run(
        body,
        name,
        (total // block,),
        [(left, spec), (right, whole(right.shape))],
        [(array((total, cols)), down_rows(block, cols))],
        needs,
    )[0]


def column_product(name, left, right, dims, block, needs=()):
    total = left.shape[1] if dims is TN else left.shape[0]
    cols = right.shape[0] if dims is NT else right.shape[1]
    spec = (
        down_rows(block, right.shape[1]) if dims is NT else along_cols(right.shape[0], block)
    )

    def body(ins, outs, _):
        outs[0][...] = dot(ins[0][...], ins[1][...], dims).astype(BF)

    return run(
        body,
        name,
        (cols // block,),
        [(left, whole(left.shape)), (right, spec)],
        [(array((total, cols)), along_cols(total, block))],
        needs,
    )[0]


def output_gradient_of(mixed, d_heads, block, needs):
    total, cols = d_heads.shape[0], d_heads.shape[1] // 2

    def body(ins, outs, _):
        outs[0][...] = dot(ins[0][...], ins[1][...], TN).astype(BF)

    return run(
        body,
        "output_gradient",
        (mixed.shape[1] // block,),
        [
            (mixed, along_cols(total, block)),
            (d_heads, pl.BlockSpec((total, cols), lambda i: (0, 1))),
        ],
        [(array((mixed.shape[1], cols)), down_rows(block, cols))],
        needs,
    )[0]


def gate_product(hats, w_gate, d_hidden, rows):
    depth, columns = w_gate.shape

    def body(ins, outs, _):
        for k in range(4):

            @pl.when(pl.program_id(0) == k)
            def _():
                outs[2][: rows // 2, :] = ins[2 * k][...]
                outs[2][rows // 2 :, :] = ins[2 * k + 1][...]

        gate = dot(outs[2][...], ins[8][...])
        outs[0][...] = gate.astype(BF)
        outs[1][...] = (ins[9][...].astype(F32) * gate * jax.nn.sigmoid(gate)).astype(BF)

    return run(
        body,
        "gate_product",
        (4,),
        [(h, whole(h.shape)) for h in hats]
        + [(w_gate, whole(w_gate.shape)), (d_hidden, down_rows(rows, columns))],
        [(array((4 * rows, cols)), down_rows(rows, cols)) for cols in (columns, columns, depth)],
    )


def up_product(chunks, hat, w_up, gate, d_hidden, rows, needs, before=()):
    columns = w_up.shape[1]
    first = chunks[0]

    def body(ins, outs, _):
        up = dot(ins[0][...], ins[1][...])
        gate = ins[2][...].astype(F32)
        sigma = jax.nn.sigmoid(gate)
        silu = gate * sigma
        outs[0][...] = (silu * up).astype(BF)
        slope = sigma + silu * (1.0 - sigma)
        outs[1][...] = (ins[3][...].astype(F32) * up * slope).astype(BF)

    spec = lambda cols: pl.BlockSpec((rows, cols), lambda i: (first + i, 0))
    ins = [
        (hat, spec(hat.shape[1])),
        (w_up, whole(w_up.shape)),
        (gate, spec(columns)),
        (d_hidden, spec(columns)),
    ]
    return run(
        body,
        "up_product",
        (len(chunks),),
        ins + [(b, ANYWHERE) for b in before],
        [(array((4 * rows, columns)), spec(columns))] * 2,
        needs,
        aliases={len(ins) + i: i for i in range(len(before))},
    )


def chunk_outs(chunks, rows, cols, block):
    outs = []
    for k in chunks:
        parts = 1 if k == 0 else 2
        outs += [(array((rows // parts, cols)), along_cols(rows // parts, block))] * parts
    return outs


def put_chunk(outs, value):
    rows = outs[0].shape[0]
    if rows == value.shape[0]:
        outs[0][...] = value.astype(BF)
        return outs[1:]
    outs[0][...] = value[:rows].astype(BF)
    outs[1][...] = value[rows:].astype(BF)
    return outs[2:]


def back_product(chunks, d_gate, d_up, w_gate, w_up, rows, needs=()):
    depth, columns = w_gate.shape
    block = depth // 4
    count = len(chunks)

    def body(ins, outs, _):
        w_one, w_two = ins[2 * count][...], ins[2 * count + 1][...]
        left = outs
        for i in range(count):
            left = put_chunk(
                left, dot(ins[i][...], w_one, NT) + dot(ins[count + i][...], w_two, NT)
            )

    return run(
        body,
        "back_first" if 3 in chunks else "back_product",
        (depth // block,),
        [(d_gate, down_rows(rows, columns, k)) for k in chunks]
        + [(d_up, down_rows(rows, columns, k)) for k in chunks]
        + [(w_gate, down_rows(block, columns)), (w_up, down_rows(block, columns))],
        chunk_outs(chunks, rows, depth, block),
        needs,
    )


def down_product(hidden, w_down, rows, needs):
    columns, depth = w_down.shape
    block = depth // 4

    def body(ins, outs, _):
        left = outs
        for k in range(4):
            left = put_chunk(left, dot(ins[0][k * rows : (k + 1) * rows, :], ins[1][...]))

    return run(
        body,
        "down_product",
        (4,),
        [(hidden, whole(hidden.shape)), (w_down, along_cols(columns, block))],
        chunk_outs(range(4), rows, depth, block),
        needs,
    )


def spans(spot, count, size):
    return [pl.ds(pl.multiple_of(spot[1 + k], 128), size) for k in range(count)]


def output_product(spot, mixes, w_outs, tokens):
    rows, depth = tokens.shape
    quarter = depth // 4
    flat = [w for pair in w_outs for w in pair]
    count = spot.shape[0] - 1

    def body(ins, outs, scratch):
        mine = ins[0][0]
        blocks = spans(ins[0], count, depth // count)
        mix, weights, x = ins[1:5], ins[5:13], ins[13]
        mixed_one, mixed_two, middle, hat_one, hat_two = outs
        mixed = scratch[0]
        half = rows // 2
        place = lambda k: pl.ds(pl.multiple_of((mine ^ k) * quarter, 128), quarter)
        for k in range(4):
            mixed[:, place(k)] = mix[k][...]
        mixed_one[...] = mixed[:half, :]
        mixed_two[...] = mixed[half:, :]
        sides = [mixed[:, block] for block in blocks]
        near = jnp.concatenate(sides[: count // 2], axis=1)
        other = jnp.concatenate(sides[count // 2 :], axis=1)
        for k in range(4):
            part = dot(near, weights[2 * k][...]) + dot(other, weights[2 * k + 1][...])
            middle[:, place(k)] = part + x[:, place(k)].astype(F32)
        value = middle[...]
        scale = lax.rsqrt(jnp.mean(value * value, axis=1, keepdims=True) + EPS)
        hat_one[...] = (value * scale)[:half].astype(BF)
        hat_two[...] = (value * scale)[half:].astype(BF)

    piece = (array((rows // 2, depth)), INSIDE)
    return run(
        body,
        "output_product",
        (),
        [(spot, SCALARS)] + [(v, INSIDE) for v in (*mixes, *flat, tokens)],
        [piece, piece, (array((rows, depth), F32), INSIDE), piece, piece],
        scratch=[pltpu.VMEM((rows, depth), BF)],
    )


def sum_parts(parts):
    own, *others = (p[...].astype(F32) for p in parts)
    return own + jnp.concatenate([others[0] + others[2], others[1] + others[3]], axis=0)


def norm_back(upstream, value):
    scale = lax.rsqrt(jnp.mean(value * value, axis=1, keepdims=True) + EPS)
    inner = jnp.mean(upstream * value, axis=1, keepdims=True)
    return scale * upstream - value * (scale * scale * scale * inner)


def middle_back(spot, parts, middle, dy, w_outs, needs):
    rows, depth = middle.shape
    quarter = depth // 4
    flat = [w for pair in w_outs for w in pair]
    count = spot.shape[0] - 1

    def body(ins, outs, scratch):
        mine = ins[0][0]
        blocks = spans(ins[0], count, depth // count)
        value, grad = ins[6:8]
        weights = ins[8:16]
        d_mixed, d_all = scratch
        upstream = sum_parts(ins[1:6])
        d_middle = grad[...].astype(F32) + norm_back(upstream, value[...])
        outs[0][...] = d_middle
        d_all[...] = d_middle.astype(BF)
        place = lambda k: pl.ds(pl.multiple_of((mine ^ k) * quarter, 128), quarter)
        near, other = 0.0, 0.0
        for k in range(4):
            part = d_all[:, place(k)]
            outs[1 + k][:, quarter:] = part
            near = near + dot(part, weights[2 * k][...], NT)
            other = other + dot(part, weights[2 * k + 1][...], NT)
        both = jnp.concatenate([near, other], axis=1).astype(BF)
        for k, block in enumerate(blocks):
            d_mixed[:, block] = both[:, k * (depth // count) : (k + 1) * (depth // count)]
        for k in range(4):
            outs[1 + k][:, :quarter] = d_mixed[:, place(k)]

    return run(
        body,
        "middle_back",
        (),
        [(spot, SCALARS)] + [(v, INSIDE) for v in (*parts, middle, dy, *flat)],
        [(array((rows, depth), F32), INSIDE)] + [(array((rows, 2 * quarter)), INSIDE)] * 4,
        needs,
        [pltpu.VMEM((rows, depth), BF), pltpu.VMEM((rows, depth), BF)],
    )


def project_back(dq, d_kv, cos_t, sin_t, weight, rows, hat, before):
    depth, wide = weight.shape
    block = depth // 4
    first = before.shape[1]

    def body(ins, outs, scratch):
        dq_ref, kv_ref, cos_ref, sin_ref, w_ref, hat_ref, before_ref = ins
        joined = scratch[0]

        @pl.when(pl.program_id(0) == 0)
        def _():
            joined[:, : wide - 128] = dq_ref[...]
            values = kv_ref[...].astype(F32)
            lane = lax.broadcasted_iota(jnp.int32, values.shape, 1)
            turned = turn(values, cos_ref[...], -sin_ref[...])
            joined[:, wide - 128 :] = jnp.where(lane < 64, turned, values).astype(BF)

        outs[0][:, :first] = before_ref[...]
        outs[0][:, first:] = dot(hat_ref[...], joined[...], TN).astype(BF)
        left = outs[1:]
        for k in range(4):
            left = put_chunk(
                left, dot(joined[k * rows : (k + 1) * rows, :], w_ref[...], NT)
            )

    return run(
        body,
        "project_back",
        (4,),
        [(v, whole(v.shape)) for v in (dq, d_kv, cos_t, sin_t)]
        + [
            (weight, down_rows(block, wide)),
            (hat, along_cols(4 * rows, block)),
            (before, down_rows(block, first)),
        ],
        [(array((depth, first + wide)), down_rows(block, first + wide))]
        + chunk_outs(range(4), rows, depth, block),
        scratch=[pltpu.VMEM((4 * rows, wide), BF)],
    )


def sum_output(parts, middle, needs):
    def body(ins, outs, _):
        outs[0][...] = (sum_parts(ins[:5]) + ins[5][...]).astype(BF)

    return run(
        body,
        "sum_output",
        (),
        [(v, INSIDE) for v in (*parts, middle)],
        [(array(middle.shape), INSIDE)],
        needs,
    )[0]


def sum_tokens(parts, tokens, d_middle, needs=()):
    def body(ins, outs, _):
        outs[0][...] = ins[6][...] + norm_back(sum_parts(ins[:5]), ins[5][...].astype(F32))

    return run(
        body,
        "sum_tokens",
        (),
        [(v, INSIDE) for v in (*parts, tokens, d_middle)],
        [(array(tokens.shape, F32), INSIDE)],
        needs,
    )[0]


def down_rows_in_order(spot, parts, needs):
    rows, cols = parts[0].shape
    if rows % 16:
        return in_order(parts, 0, F32)

    def body(ins, outs, _):
        for k in range(4):
            first = pl.multiple_of((ins[0][0] ^ k) * rows, 16)
            outs[0][pl.ds(first, rows), :] = ins[1 + k][...].astype(F32)

    return run(
        body,
        "finish",
        (),
        [(spot, SCALARS)] + [(v, INSIDE) for v in parts],
        [(array((4 * rows, cols), F32), INSIDE)],
        needs,
    )[0]


def finish_attention(mine, parts, gain, output, query, key, value):
    rows, depth = output.shape
    quarter, wide = depth // 4, query.shape[1] // 4
    weights = (query, key, value)

    def body(ins, outs, scratch):
        scale, total = ins[5][...], 0.0
        joined = scratch[0]
        for k in range(4):
            joined[ins[0][0] ^ k] = ins[1 + k][...]
        begin = 0
        for i, size in enumerate((quarter, wide, HEAD_DIM, HEAD_DIM)):
            raw = jnp.concatenate(
                [joined[k][:, begin : begin + size].astype(F32) for k in range(4)], axis=1
            )
            begin += size
            if i == 0:
                outs[0][...] = raw
            else:
                weight = ins[5 + i][...].astype(F32)
                total = total + jnp.sum(raw * weight, axis=1, keepdims=True)
                outs[i][...] = raw * scale
        outs[4][...] = total

    return run(
        body,
        "finish",
        (),
        [(mine, SCALARS)] + [(v, INSIDE) for v in (*parts, gain, *weights)],
        [(array(w.shape, F32), INSIDE) for w in (output, *weights)]
        + [(array((rows, 1), F32), INSIDE)],
        scratch=[pltpu.VMEM((4, rows, parts[0].shape[1]), BF)],
    )


def hop(value, step):
    return lax.ppermute(value, "dp", [(i, i ^ step) for i in range(4)])


def gather_halves(one, two, hold=()):
    next_two, other_one = hop(two, 1), hop(one, 2)
    next_one, other_two = hop(one, 1), hop(two, 2)
    if hold:
        hold = (*hold, next_one, other_two)
        next_two, other_one = tie(next_two, *hold), tie(other_one, *hold)
    far = [hop(other_one, 1), hop(next_two, 2)]
    return [one, two, next_one, next_two, other_one, other_two, *far]


def gather_plane(value, hold=()):
    half = value.shape[0] // 2
    one = hop(value, 1)
    two = hop(value, 2)
    if hold:
        one, two = tie(one, *hold), tie(two, *hold)
    return [value, one, two, hop(two[:half], 1), hop(one[half:], 2)]


def join(parts):
    return jnp.concatenate(parts, axis=0)


def gather_direct(value):
    return [value] + [hop(value, k) for k in range(1, 4)]


def reduce_first(parts):
    return hop(parts[5], 1), hop(parts[6], 2)


def reduce_plain(parts, hold=None):
    one_a, two_b = parts[1], parts[4]
    if hold is not None:
        one_a, two_b = tie(one_a, hold), tie(two_b, hold)
    return hop(one_a, 1), hop(two_b, 2)


def reduce_second(parts, came, needs=()):
    own, _, one_b, two_a = parts[:4]
    by_one, by_two, next_a, other_b = came

    def body(ins, outs, _):
        for k in range(2):
            outs[k][...] = (ins[k][...].astype(F32) + ins[2 + k][...].astype(F32)).astype(BF)

    one_b, two_a = run(
        body,
        "merge",
        (),
        [(v, INSIDE) for v in (one_b, two_a, by_two, by_one)],
        [(array(one_b.shape), INSIDE)] * 2,
        needs,
    )
    return one_b, (own, next_a, hop(one_b, 1), hop(two_a, 2), other_b)


def core_swap(value):
    size = lax.axis_size("seq")
    return lax.ppermute(value, "seq", [(i, i ^ 1) for i in range(size)])


def in_order(parts, axis, dtype=None):
    mine = lax.axis_index("dp")
    shape = list(parts[0].shape)
    size = shape[axis]
    shape[axis] = 4 * size
    out = jnp.zeros(shape, dtype or parts[0].dtype)
    for k, part in enumerate(parts):
        out = lax.dynamic_update_slice_in_dim(
            out, part.astype(out.dtype), (mine ^ k) * size, axis
        )
    return out


def local(
    tokens,
    lengths,
    attention_gain,
    query_weight,
    key_weight,
    value_weight,
    output_weight,
    feedforward_gain,
    gate_weight,
    up_weight,
    down_weight,
    cotangent,
):
    rows, depth = tokens.shape
    shards = lax.axis_size("seq")
    mine = lax.axis_index("dp")
    place = lax.axis_index("seq")
    core = place % 2
    wide = HEADS // KV_HEADS * HEAD_DIM
    side = depth // 2
    near = lambda v: lax.all_gather(v, "seq", axis=0, tiled=True)
    far = lambda v: lax.psum_scatter(v, "seq", scatter_dimension=0, tiled=True)

    gain_a = attention_gain.astype(F32)[:, None]
    gain_f = feedforward_gain.astype(F32)[:, None]
    own_qkv = jnp.concatenate(
        [
            lax.dynamic_slice_in_dim(query_weight, mine * wide, wide, 1),
            lax.dynamic_slice_in_dim(key_weight, mine * HEAD_DIM, HEAD_DIM, 1),
            lax.dynamic_slice_in_dim(value_weight, mine * HEAD_DIM, HEAD_DIM, 1),
        ],
        axis=1,
    )
    w_qkv = near((own_qkv.astype(F32) * gain_a).astype(BF))
    own_block = lax.dynamic_slice_in_dim(
        output_weight, mine * (depth // 4), depth // 4, 1
    )
    sizes = join([lengths] + [hop(lengths, k) for k in range(1, 4)])
    xs = gather_plane(tokens)
    own_out = near(tie(own_block, w_qkv, xs[1], xs[2], sizes))
    spot = jnp.stack([mine, core * side, (1 - core) * side])
    piece = down_weight.shape[0] // 4
    w_down = near(lax.dynamic_slice_in_dim(down_weight, mine * piece, piece, 0))
    own_gate, own_up = pick_columns(mine[None], gain_f, gate_weight, up_weight, shards)
    w_gate = near(own_gate)
    w_up = near(own_up)

    count = sizes.shape[1]
    before = jnp.arange(count)[:, None] <= jnp.arange(count)[None, :]
    ends = jnp.sum(jnp.where(before[None], sizes[:, :, None], 0), axis=1)
    index = place * rows + jnp.arange(rows, dtype=jnp.int32)
    passed = ends[:, None, :] <= index[None, :, None]
    begin = jnp.max(jnp.where(passed, ends[:, None, :], 0), axis=2)
    position = (index[None, :] - begin).astype(F32).reshape(4 * rows)
    half = HEAD_DIM // 2
    inverse = ROPE_BASE ** (-jnp.arange(half, dtype=F32) * 2.0 / HEAD_DIM)
    theta = position[:, None] * inverse[None, :]
    cos_h, sin_h = jnp.cos(theta), jnp.sin(theta)
    cos_t = jnp.concatenate([cos_h] * 4, axis=1)
    sin_t = jnp.concatenate([-sin_h, sin_h] * 2, axis=1)
    bounds = jnp.stack([begin, jnp.broadcast_to(index[None, :], begin.shape)], axis=1)
    bounds = jnp.concatenate([bounds] * (wide // HEAD_DIM), axis=2)
    low = begin[:, 0] // rows
    split = jnp.clip((begin[:, rows - 1] + rows - 1) // rows, low, place)
    where = jnp.concatenate([low, split, place[None]])

    made = ()
    for k, pieces in enumerate((xs[0:1], xs[1:2], xs[2:3], xs[3:5])):
        made = project(k, pieces, w_qkv, cos_t, sin_t, rows, made)
    hat, queries, own_kv = made
    own_half, own_rest = (
        lax.dynamic_slice_in_dim(own_out, c * side, side, 0) for c in (core, 1 - core)
    )
    kv = lax.all_gather(tie(own_kv, own_half), "seq", axis=0)
    own_half = tie(own_half, xs[3], xs[4])
    own_half, got_one, got_two, far_one, far_two = gather_plane(own_half)
    got = [own_half, got_one, got_two]
    swapped = [own_rest, core_swap(got_one), core_swap(got_two)]
    dy_own = tie(cotangent, got_one, got_two)
    dy_one, dy_two = hop(dy_own, 1), hop(dy_own, 2)
    mixed_heads, lse = attend(
        where, queries, kv, bounds, rows, (got_one, got_two, *swapped[1:])
    )
    mixed_heads = tie(mixed_heads, far_one, far_two, dy_one, dy_two)
    got.append(join([tie(far_one, mixed_heads), far_two]))
    swapped.append(core_swap(got[3]))
    w_outs = list(zip(got, swapped, strict=True))
    mixes = [mixed_heads[:rows]] + [
        hop(mixed_heads[k * rows : (k + 1) * rows], k) for k in range(1, 4)
    ]
    mixed_one, mixed_two, middle, hat_one, hat_two = output_product(
        spot, mixes, w_outs, tokens
    )

    part = rows // 2
    dy_far = hop(tie(dy_two[:part], *mixes), 1), hop(tie(dy_one[part:], *mixes), 2)
    dy_all = join([tie(dy_own, hat_one), dy_one, dy_two, *dy_far])
    d_hidden = row_product("hidden_back", dy_all, w_down, NT, rows, (hat_two,))
    hats = gather_halves(hat_one, hat_two, (d_hidden,))
    mixes_all = gather_halves(tie(mixed_one, *hats[6:]), tie(mixed_two, *hats[6:]))
    gate, d_up, hat_all = gate_product(hats, w_gate, d_hidden, rows)
    up_raw = row_product("up_gradient", hat_all, d_up, TN, wide)
    up_part = far(up_raw)
    ups_of = functools.partial(
        up_product, hat=hat_all, w_up=w_up, gate=gate, d_hidden=d_hidden, rows=rows
    )
    back = functools.partial(back_product, d_up=d_up, w_gate=w_gate, w_up=w_up, rows=rows)
    some = ups_of((3,), needs=(up_raw, *mixes_all[2:6]))
    far_one, far_two = back((3,), d_gate=some[1], needs=mixes_all[6:])
    hidden, d_gate = ups_of((0, 1, 2), needs=(far_one,), before=some)
    came = reduce_first([None] * 5 + [far_one, far_two])
    down_raw = column_product("down_gradient", hidden, dy_all, TN, wide)
    down_part = far(down_raw)
    sides = back((1, 2), d_gate=d_gate, needs=(down_raw, *came))
    came += reduce_plain((None, *sides))
    first, terms = reduce_second((None, *sides), came)
    (d_own,) = back((0,), d_gate=d_gate, needs=(first,))
    terms = (d_own, *terms[1:])
    mixed_all = join(mixes_all)
    d_middle, *blocks = middle_back(
        spot, terms, middle, cotangent, w_outs, (up_part, mixed_all)
    )

    d_heads = join([blocks[0]] + [hop(blocks[k], k) for k in range(1, 4)])
    gate_raw = row_product("gate_gradient", hat_all, d_gate, TN, wide, (blocks[0],))
    gate_part = far(gate_raw)
    outs = down_product(hidden, w_down, rows, (gate_raw,))
    ups_one, ups_two = hop(up_part, 1), hop(up_part, 2)
    dq, dkv = attend_back(
        where, queries, kv, bounds, d_heads, mixed_heads, lse, cos_t, sin_t, rows, (outs[6], ups_one, ups_two)
    )
    came = reduce_first(outs)
    downs_one, downs_two = hop(down_part, 1), hop(down_part, 2)
    ups_far = hop(up_part, 3)
    dkv = tie(dkv, gate_part, *came, downs_one, downs_two, ups_far)
    came += reduce_plain(outs, dkv)
    own_dkv = far(dkv.reshape(shards * 4 * rows, 128))
    first, terms = reduce_second(outs, came, (dkv,))
    out_raw = output_gradient_of(mixed_all, d_heads, wide, (first,))
    downs_far = hop(tie(down_part, dkv), 3)
    own_dkv = tie(own_dkv, out_raw, *terms[1:], downs_far)
    both_raw, *fs = project_back(
        dq, own_dkv, cos_t, sin_t, w_qkv, rows, hat, out_raw
    )
    both_part = far(both_raw)
    layer_output = sum_output(terms, middle, (fs[6],))
    came = (*reduce_first(fs), *reduce_plain(fs))
    first, terms = reduce_second(fs, came, came[2:])
    gates = gather_plane(tie(gate_part, first), (both_part,))
    token_gradient = sum_tokens(terms, tokens, d_middle)

    gate_gradient, gain_g = spread_columns(
        "spread_gate",
        mine[None],
        jnp.stack([*gates[:3], join(gates[3:])]),
        gain_f,
        gate_weight,
        shards,
    )
    up_gradient, gain_u = spread_columns(
        "spread_up", mine[None], jnp.stack([tie(up_part, both_raw), ups_one, ups_two, ups_far]), gain_f, up_weight, shards
    )
    down_gradient = down_rows_in_order(
        spot, [down_part, downs_one, downs_two, downs_far], (both_raw,)
    )
    gradients = finish_attention(
        mine[None],
        gather_direct(both_part),
        gain_a,
        output_weight,
        query_weight,
        key_weight,
        value_weight,
    )
    output_gradient, query_gradient, key_gradient, value_gradient, gain_a_gradient = gradients
    return (
        layer_output,
        token_gradient,
        gain_a_gradient[:, 0],
        query_gradient,
        key_gradient,
        value_gradient,
        output_gradient,
        (gain_g + gain_u)[:, 0],
        gate_gradient,
        up_gradient,
        down_gradient,
    )


def solution(mesh):
    both = P(("dp", "seq"), None)
    flat = P("seq")
    split = P("seq", None)
    return jax.shard_map(
        local,
        mesh=mesh,
        in_specs=(
            both,
            P("dp", None),
            flat,
            split,
            split,
            split,
            split,
            flat,
            split,
            split,
            split,
            both,
        ),
        out_specs=(
            both,
            both,
            flat,
            split,
            split,
            split,
            split,
            flat,
            split,
            split,
            split,
        ),
        check_vma=False,
    )
```

profile of v0, /device:TPU:28, one launch (start us, length us, event | category | flops | bytes accessed | tf_op | source)
XLA Modules:
  0.0 684.5 jit_solution(6560574908059236919)
XLA Ops:
  18.2 24.9 %collective-permute-done.1 = s32[1,2]{1,0:T(1,128)S(1)} collective-permute-done((s32[1,2]{1,0:T(1,128)}, s32[1,2]{1,0:T(1,128)S(1)}, u32[]{:S(2)}, u32[]{:S(2)}) %collective-permute-start.1) | collective-permute-done | bytes 40 | tf_op jit(solution)/shard_map/ppermute | solution.py:863
  87.1 23.2 %collective-permute-done.8.rest_1_.refs_2_.refs_9_.refs_12_ = bf16[1024,512]{1,0:T(8,128)(2,1)S(1)} collective-permute-done((bf16[1024,512]{1,0:T(8,128)(2,1)}, bf16[1024,512]{1,0:T(8,128)(2,1)S(1)}, u32[]{:S(2)}, u32[]{:S(2)}) %collective-permute-start.8) | collective-permute-done | bytes 1048608 | tf_op jit(solution)/shard_map/ppermute | solution.py:863
  123.4 29.2 %attend.1 = (bf16[1280,512]{1,0:T(8,128)(2,1)}, f32[4,1,2560]{2,1,0:T(1,128)}) custom-call(s32[9]{0:T(128)} %pad_add_fusion.3.where, bf16[1280,512]{1,0:T(8,128)(2,1)} %get-tuple-element.91.q_ref, bf16[8,1280,128]{2,1,0:T(8,128)(2,1)} %bitcast.23, s32[4,2,2560]{2,1,0:T(2,128)} %concatenate.38.bound_ref, bf16[1024,512]{1,0:T(8,128)(2,1)} %copy-done.4, ...), custom_call_target="tpu_custom_call" | custom-call | flops 320000000000 | bytes 1000000000 | tf_op jit(solution)/shard_map/attend/pallas_call | solution.py:326
  173.0 6.4 collective-permute-done.16.refs_3_
  182.2 10.3 %output_product.1 = (bf16[160,2048]{1,0:T(8,128)(2,1)}, bf16[160,2048]{1,0:T(8,128)(2,1)}, f32[320,2048]{1,0:T(8,128)}, bf16[160,2048]{1,0:T(8,128)(2,1)}, bf16[160,2048]{1,0:T(8,128)(2,1)}) custom-call(s32[3]{0:T(128)} %pad_add_fusion.2.refs_0_, bf16[320,512]{1,0:T(8,128)(2,1)} %get-tuple-element.164.refs_1_, bf16[320,512]{1,0:T(8,128)(2,1)} %copy-done.18, ...), custom_call_target="tpu_custom_call" | custom-call | flops 2400000000 | bytes 7500000 | tf_op jit(solution)/shard_map/output_product/pallas_call | solution.py:97
  209.5 13.0 %hidden_back.1.refs_1_.refs_9_.refs_3_ = bf16[1280,1408]{1,0:T(8,128)(2,1)} custom-call(bf16[1280,2048]{1,0:T(8,128)(2,1)} %constant_dynamic-update-slice_fusion.refs_0_.refs_1_, bf16[1408,2048]{1,0:T(8,128)(2,1)} %all-gather.12.cloned.1.call-done.refs_1_, bf16[160,2048]{1,0:T(8,128)(2,1)} %get-tuple-element.95.refs_2_.refs_1_), custom_call_target="tpu_custom_call" | custom-call | flops 3200000000 | bytes 10000000 | tf_op jit(solution)/shard_map/hidden_back/pallas_call | solution.py:97
  230.2 12.5 %collective-permute-done.26.refs_7_.refs_2_ = bf16[160,2048]{1,0:T(8,128)(2,1)S(1)} collective-permute-done((bf16[160,2048]{1,0:T(8,128)(2,1)}, bf16[160,2048]{1,0:T(8,128)(2,1)S(1)}, u32[]{:S(2)}, u32[]{:S(2)}) %collective-permute-start.26) | collective-permute-done | bytes 655392 | tf_op jit(solution)/shard_map/ppermute | solution.py:863
  249.9 15.8 %gate_product.1 = (bf16[1280,1408]{1,0:T(8,128)(2,1)}, bf16[1280,1408]{1,0:T(8,128)(2,1)}, bf16[1280,2048]{1,0:T(8,128)(2,1)}) custom-call(bf16[160,2048]{1,0:T(8,128)(2,1)} %get-tuple-element.94.refs_1_.refs_0_, bf16[160,2048]{1,0:T(8,128)(2,1)} %get-tuple-element.95.refs_2_.refs_1_, bf16[160,2048]{1,0:T(8,128)(2,1)} %copy-done.6, ...), custom_call_target="tpu_custom_call" | custom-call | flops 1600000000 | bytes 5000000 | tf_op jit(solution)/shard_map/gate_product/pallas_call | solution.py:97
  265.7 12.9 %up_gradient.1.refs_4_ = bf16[2048,1408]{1,0:T(8,128)(2,1)} custom-call(bf16[1280,2048]{1,0:T(8,128)(2,1)} %get-tuple-element.97.refs_0_, bf16[1280,1408]{1,0:T(8,128)(2,1)} %get-tuple-element.100.refs_1_.refs_2_.refs_3_), custom_call_target="tpu_custom_call" | custom-call | flops 1600000000 | bytes 5000000 | tf_op jit(solution)/shard_map/up_gradient/pallas_call | solution.py:97
  283.6 9.6 %all-gather.16.cloned.1.call-done.refs_1_.refs_3_.refs_5_ = bf16[2048,1408]{1,0:T(8,128)(2,1)} async-done(((bf16[256,1408]{1,0:T(8,128)(2,1)}), bf16[2048,1408]{1,0:T(8,128)(2,1)}) %all-gather.16.cloned.1.call-update) | async-done | bytes 5767184 | tf_op jit(solution)/shard_map/all_gather | solution.py:962
  293.2 7.0 %up_product.2 = (bf16[1280,1408]{1,0:T(8,128)(2,1)}, bf16[1280,1408]{1,0:T(8,128)(2,1)}) custom-call(bf16[1280,2048]{1,0:T(8,128)(2,1)} %get-tuple-element.97.refs_0_, bf16[2048,1408]{1,0:T(8,128)(2,1)} %all-gather.16.cloned.1.call-done.refs_1_.refs_3_.refs_5_, bf16[1280,1408]{1,0:T(8,128)(2,1)} %get-tuple-element.99.refs_2_, ...), custom_call_target="tpu_custom_call" | custom-call | flops 80000000000 | bytes 250000000 | tf_op jit(solution)/shard_map/up_product/pallas_call | solution.py:97
  308.3 8.9 %back_first.1 = (bf16[160,2048]{1,0:T(8,128)(2,1)}, bf16[160,2048]{1,0:T(8,128)(2,1)}) custom-call(bf16[1280,1408]{1,0:T(8,128)(2,1)} %get-tuple-element.104.refs_0_.refs_5_, bf16[1280,1408]{1,0:T(8,128)(2,1)} %get-tuple-element.100.refs_1_.refs_2_.refs_3_, bf16[2048,1408]{1,0:T(8,128)(2,1)} %all-gather.14.cloned.1.call-done.refs_8_.refs_2_.refs_4_, ...), custom_call_target="tpu_custom_call" | custom-call | flops 3200000000 | bytes 10000000 | tf_op jit(solution)/shard_map/back_first/pallas_call | solution.py:97
  319.2 12.4 %up_product.3 = (bf16[1280,1408]{1,0:T(8,128)(2,1)}, bf16[1280,1408]{1,0:T(8,128)(2,1)}) custom-call(bf16[1280,2048]{1,0:T(8,128)(2,1)} %get-tuple-element.97.refs_0_, bf16[2048,1408]{1,0:T(8,128)(2,1)} %all-gather.16.cloned.1.call-done.refs_1_.refs_3_.refs_5_, ...), custom_call_target="tpu_custom_call", output_to_operand_aliasing={{0}: (4, {}), {1}: (5, {})} | custom-call | flops 80000000000 | bytes 250000000 | tf_op jit(solution)/shard_map/up_product/pallas_call | solution.py:97
  331.6 11.9 %down_gradient.1.refs_6_ = bf16[1408,2048]{1,0:T(8,128)(2,1)} custom-call(bf16[1280,1408]{1,0:T(8,128)(2,1)} %get-tuple-element.106.refs_0_, bf16[1280,2048]{1,0:T(8,128)(2,1)} %constant_dynamic-update-slice_fusion.refs_0_.refs_1_), custom_call_target="tpu_custom_call" | custom-call | flops 160000000 | bytes 500000 | tf_op jit(solution)/shard_map/down_gradient/pallas_call | solution.py:97
  344.7 12.8 %back_product.2 = (bf16[160,2048]{1,0:T(8,128)(2,1)}, bf16[160,2048]{1,0:T(8,128)(2,1)}, bf16[160,2048]{1,0:T(8,128)(2,1)}, bf16[160,2048]{1,0:T(8,128)(2,1)}) custom-call(bf16[1280,1408]{1,0:T(8,128)(2,1)} %get-tuple-element.107.refs_0_.refs_1_, bf16[1280,1408]{1,0:T(8,128)(2,1)} %get-tuple-element.107.refs_0_.refs_1_, ...), custom_call_target="tpu_custom_call" | custom-call | flops 3200000000 | bytes 10000000 | tf_op jit(solution)/shard_map/back_product/pallas_call | solution.py:97
  366.6 8.8 %back_product.3.refs_1_ = bf16[320,2048]{1,0:T(8,128)(2,1)} custom-call(bf16[1280,1408]{1,0:T(8,128)(2,1)} %get-tuple-element.107.refs_0_.refs_1_, bf16[1280,1408]{1,0:T(8,128)(2,1)} %get-tuple-element.100.refs_1_.refs_2_.refs_3_, bf16[2048,1408]{1,0:T(8,128)(2,1)} %all-gather.14.cloned.1.call-done.refs_8_.refs_2_.refs_4_, ...), custom_call_target="tpu_custom_call" | custom-call | flops 3200000000 | bytes 10000000 | tf_op jit(solution)/shard_map/back_product/pallas_call | solution.py:97
  380.0 12.4 %collective-permute-done.35.refs_2_ = bf16[160,2048]{1,0:T(8,128)(2,1)S(1)} collective-permute-done((bf16[160,2048]{1,0:T(8,128)(2,1)S(1)}, bf16[160,2048]{1,0:T(8,128)(2,1)S(1)}, u32[]{:S(2)}, u32[]{:S(2)}) %collective-permute-start.35) | collective-permute-done | bytes 655392 | tf_op jit(solution)/shard_map/ppermute | solution.py:863
  393.3 12.0 %middle_back.1 = (f32[320,2048]{1,0:T(8,128)}, bf16[320,1024]{1,0:T(8,128)(2,1)}, bf16[320,1024]{1,0:T(8,128)(2,1)}, bf16[320,1024]{1,0:T(8,128)(2,1)}, bf16[320,1024]{1,0:T(8,128)(2,1)}) custom-call(s32[3]{0:T(128)} %pad_add_fusion.2.refs_0_, bf16[320,2048]{1,0:T(8,128)(2,1)} %back_product.3.refs_1_, bf16[160,2048]{1,0:T(8,128)(2,1)} %copy-done.51, ...), custom_call_target="tpu_custom_call" | custom-call | flops 160000000000 | bytes 500000000 | tf_op jit(solution)/shard_map/middle_back/pallas_call | solution.py:97
  409.7 12.6 %gate_gradient.1.refs_2_ = bf16[2048,1408]{1,0:T(8,128)(2,1)} custom-call(bf16[1280,2048]{1,0:T(8,128)(2,1)} %get-tuple-element.97.refs_0_, bf16[1280,1408]{1,0:T(8,128)(2,1)} %get-tuple-element.107.refs_0_.refs_1_, bf16[320,1024]{1,0:T(8,128)(2,1)} %get-tuple-element.116.refs_2_), custom_call_target="tpu_custom_call" | custom-call | flops 1600000000 | bytes 5000000 | tf_op jit(solution)/shard_map/gate_gradient/pallas_call | solution.py:97
  422.4 12.4 %down_product.1 = (bf16[320,2048]{1,0:T(8,128)(2,1)}, bf16[160,2048]{1,0:T(8,128)(2,1)}, bf16[160,2048]{1,0:T(8,128)(2,1)}, bf16[160,2048]{1,0:T(8,128)(2,1)}, b...) custom-call(bf16[1280,1408]{1,0:T(8,128)(2,1)} %get-tuple-element.106.refs_0_, ...), custom_call_target="tpu_custom_call" | custom-call | flops 3200000000 | bytes 10000000 | tf_op jit(solution)/shard_map/down_product/pallas_call | solution.py:97
  443.2 10.2 %collective-permute-done.43.rest_2_ = bf16[256,1408]{1,0:T(8,128)(2,1)} collective-permute-done((bf16[256,1408]{1,0:T(8,128)(2,1)}, bf16[256,1408]{1,0:T(8,128)(2,1)}, u32[]{:S(2)}, u32[]{:S(2)}) %collective-permute-start.43) | collective-permute-done | bytes 720928 | tf_op jit(solution)/shard_map/ppermute | solution.py:863
  455.3 42.7 %attend_back.1 = (bf16[1280,512]{1,0:T(8,128)(2,1)}, bf16[8,1280,128]{2,1,0:T(8,128)(2,1)}) custom-call(s32[9]{0:T(128)} %pad_add_fusion.3.where, bf16[1280,512]{1,0:T(8,128)(2,1)} %get-tuple-element.91.q_ref, bf16[8,1280,128]{2,1,0:T(8,128)(2,1)} %bitcast.24, s32[4,2,2560]{2,1,0:T(2,128)} %concatenate.38.bound_ref, bf16[1280,1024]{1,0:T(8,128)(2,1)} %copy-done.15, ...), custom_call_target="tpu_custom_call" | custom-call | flops 799999983616 | bytes 2500000000 | tf_op jit(solution)/shard_map/attend_back/pallas_call | solution.py:432
  509.4 7.0 %output_gradient.1.refs_1_.refs_6_ = bf16[2048,512]{1,0:T(8,128)(2,1)} custom-call(bf16[1280,2048]{1,0:T(8,128)(2,1)} %constant_dynamic-update-slice_fusion.5.refs_17_.refs_0_, bf16[1280,1024]{1,0:T(8,128)(2,1)} %copy-done.15, bf16[160,2048]{1,0:T(8,128)(2,1)} %get-tuple-element.128.refs_2_), custom_call_target="tpu_custom_call" | custom-call | flops 1600000000 | bytes 5000000 | tf_op jit(solution)/shard_map/output_gradient/pallas_call | solution.py:97
  516.5 29.5 %collective-permute-done.51.refs_4_.refs_3_ = bf16[160,2048]{1,0:T(8,128)(2,1)S(1)} collective-permute-done((bf16[160,2048]{1,0:T(8,128)(2,1)}, bf16[160,2048]{1,0:T(8,128)(2,1)S(1)}, u32[]{:S(2)}, u32[]{:S(2)}) %collective-permute-start.51) | collective-permute-done | bytes 655392 | tf_op jit(solution)/shard_map/ppermute | solution.py:863
  547.1 13.7 %project_back.1 = (bf16[2048,1152]{1,0:T(8,128)(2,1)}, bf16[320,2048]{1,0:T(8,128)(2,1)}, bf16[160,2048]{1,0:T(8,128)(2,1)}, bf16[160,2048]{1,0:T(8,128)(2,1)}, ...) custom-call(bf16[1280,512]{1,0:T(8,128)(2,1)} %get-tuple-element.131, ...), custom_call_target="tpu_custom_call" | custom-call | flops 1600000000 | bytes 5000000 | tf_op jit(solution)/shard_map/project_back/pallas_call | solution.py:97
  568.1 6.8 spread_up.1
  578.2 14.0 %collective-permute-done.56.refs_3_ = bf16[160,2048]{1,0:T(8,128)(2,1)} collective-permute-done((bf16[160,2048]{1,0:T(8,128)(2,1)}, bf16[160,2048]{1,0:T(8,128)(2,1)}, u32[]{:S(2)}, u32[]{:S(2)}) %collective-permute-start.56) | collective-permute-done | bytes 655392 | tf_op jit(solution)/shard_map/ppermute | solution.py:863
  611.2 7.5 %collective-permute-done.64.refs_0_ = bf16[256,1408]{1,0:T(8,128)(2,1)S(1)} collective-permute-done((bf16[256,1408]{1,0:T(8,128)(2,1)}, bf16[256,1408]{1,0:T(8,128)(2,1)S(1)}, u32[]{:S(2)}, u32[]{:S(2)}) %collective-permute-start.64) | collective-permute-done | bytes 720928 | tf_op jit(solution)/shard_map/ppermute | solution.py:863
  621.0 10.0 %collective-permute-done.63.refs_0_ = bf16[256,1408]{1,0:T(8,128)(2,1)S(1)} collective-permute-done((bf16[256,1408]{1,0:T(8,128)(2,1)}, bf16[256,1408]{1,0:T(8,128)(2,1)S(1)}, u32[]{:S(2)}, u32[]{:S(2)}) %collective-permute-start.63) | collective-permute-done | bytes 720928 | tf_op jit(solution)/shard_map/ppermute | solution.py:863
  635.7 6.5 sum_tokens.1
  647.6 6.8 spread_gate.1
  659.4 9.9 %collective-permute-done.61.refs_3_ = bf16[256,1152]{1,0:T(8,128)(2,1)S(1)} collective-permute-done((bf16[256,1152]{1,0:T(8,128)(2,1)S(1)}, bf16[256,1152]{1,0:T(8,128)(2,1)S(1)}, u32[]{:S(2)}, u32[]{:S(2)}) %collective-permute-start.61) | collective-permute-done | bytes 589856 | tf_op jit(solution)/shard_map/ppermute | solution.py:863
  (368 shorter events, 235.7 us)
Async XLA Ops:
  7.2 37.2 %all-gather.8.cloned.1.call-start = ((), (), s32[]{:S(2)}) async-start(), calls=%async_computation.5 | async-start | bytes 2949120 | tf_op jit(solution)/shard_map/all_gather | solution.py:962
  10.9 63.9 %all-gather.10.cloned.1.call-start = ((), (), s32[]{:S(2)}) async-start(), calls=%async_computation.6 | async-start | bytes 2359296 | tf_op jit(solution)/shard_map/all_gather | solution.py:962
  44.4 79.0 %all-gather.18.cloned.1.call-start = ((), (), s32[]{:S(2)}) async-start(), calls=%async_computation.15 | async-start | bytes 2949120 | tf_op jit(solution)/shard_map/all_gather | solution.py:1015
  77.9 131.6 %all-gather.12.cloned.1.call-start = ((), (), s32[]{:S(2)}) async-start(), calls=%async_computation.7 | async-start | bytes 6488064 | tf_op jit(solution)/shard_map/all_gather | solution.py:962
  78.9 171.0 %all-gather.14.cloned.1.call-start = ((), (), s32[]{:S(2)}) async-start(), calls=%async_computation.8 | async-start | bytes 6488064 | tf_op jit(solution)/shard_map/all_gather | solution.py:962
  84.8 208.4 %all-gather.16.cloned.1.call-start = ((), (), s32[]{:S(2)}) async-start(), calls=%async_computation.9 | async-start | bytes 6488064 | tf_op jit(solution)/shard_map/all_gather | solution.py:962
  110.8 281.6 %reduce-scatter.6.cloned.1.call-start = ((), (), s32[]{:S(2)}) async-start(), calls=%async_computation.10 | async-start | bytes 6488064 | tf_op jit(solution)/shard_map/reduce_scatter | solution.py:963
  115.6 43.5 %collective-permute-start.14 = (bf16[320,2048]{1,0:T(8,128)(2,1)}, bf16[320,2048]{1,0:T(8,128)(2,1)}, u32[]{:S(2)}, u32[]{:S(2)}) collective-permute-start(bf16[320,2048]{1,0:T(8,128)(2,1)} %tie.25.refs_0_), channel_id=1, source_target_pairs={{0,16},{8,24},{16,0},{24,8},{1,17},{9,25},{17,1},{25,9},{2,18},{10... | collective-permute-start | bytes 3932168 | tf_op jit(solution)/shard_map/ppermute | solution.py:863
  116.9 42.2 %collective-permute-start.13 = (bf16[320,2048]{1,0:T(8,128)(2,1)}, bf16[320,2048]{1,0:T(8,128)(2,1)}, u32[]{:S(2)}, u32[]{:S(2)}) collective-permute-start(bf16[320,2048]{1,0:T(8,128)(2,1)} %tie.25.refs_0_), channel_id=1, source_target_pairs={{0,8},{8,0},{16,24},{24,16},{1,9},{9,1},{17,25},{25,17},{2,10},{10... | collective-permute-start | bytes 3932168 | tf_op jit(solution)/shard_map/ppermute | solution.py:863
  120.1 39.0 %collective-permute-start.11 = (bf16[512,512]{1,0:T(8,128)(2,1)}, bf16[512,512]{1,0:T(8,128)(2,1)}, u32[]{:S(2)}, u32[]{:S(2)}) collective-permute-start(bf16[512,512]{1,0:T(8,128)(2,1)} %slice.60), channel_id=1, source_target_pairs={{0,8},{8,0},{16,24},{24,16},{1,9},{9,1},{17,25},{25,17},{2,10},{10... | collective-permute-start | bytes 1572872 | tf_op jit(solution)/shard_map/ppermute | solution.py:863
  122.7 36.3 %collective-permute-start.12 = (bf16[512,512]{1,0:T(8,128)(2,1)}, bf16[512,512]{1,0:T(8,128)(2,1)}, u32[]{:S(2)}, u32[]{:S(2)}) collective-permute-start(bf16[512,512]{1,0:T(8,128)(2,1)} %slice.61), channel_id=1, source_target_pairs={{0,16},{8,24},{16,0},{24,8},{1,17},{9,25},{17,1},{25,9},{2,18},{10... | collective-permute-start | bytes 1572872 | tf_op jit(solution)/shard_map/ppermute | solution.py:863
  193.7 34.9 %collective-permute-start.24 = (bf16[160,2048]{1,0:T(8,128)(2,1)S(1)}, bf16[160,2048]{1,0:T(8,128)(2,1)S(1)}, u32[]{:S(2)}, u32[]{:S(2)}) collective-permute-start(bf16[160,2048]{1,0:T(8,128)(2,1)S(1)} %copy-done.30), channel_id=1, source_target_pairs={{0,16},{8,24},{16,0},{24,8},{1,17},{9,25},{17,1},{25,9},{2,18},{10... | collective-permute-start | bytes 1966088 | tf_op jit(solution)/shard_map/ppermute | solution.py:863
  245.9 35.7 %collective-permute-start.29 = (bf16[160,2048]{1,0:T(8,128)(2,1)}, bf16[160,2048]{1,0:T(8,128)(2,1)S(1)}, u32[]{:S(2)}, u32[]{:S(2)}) collective-permute-start(bf16[160,2048]{1,0:T(8,128)(2,1)} %tie.33), channel_id=1, source_target_pairs={{0,16},{8,24},{16,0},{24,8},{1,17},{9,25},{17,1},{25,9},{2,18},{10... | collective-permute-start | bytes 1966088 | tf_op jit(solution)/shard_map/ppermute | solution.py:863
  246.2 47.0 %collective-permute-start.27 = (bf16[160,2048]{1,0:T(8,128)(2,1)}, bf16[160,2048]{1,0:T(8,128)(2,1)}, u32[]{:S(2)}, u32[]{:S(2)}) collective-permute-start(bf16[160,2048]{1,0:T(8,128)(2,1)} %tie.33), channel_id=1, source_target_pairs={{0,8},{8,0},{16,24},{24,16},{1,9},{9,1},{17,25},{25,17},{2,10},{10... | collective-permute-start | bytes 1966088 | tf_op jit(solution)/shard_map/ppermute | solution.py:863
  247.9 45.3 %collective-permute-start.30 = (bf16[160,2048]{1,0:T(8,128)(2,1)}, bf16[160,2048]{1,0:T(8,128)(2,1)}, u32[]{:S(2)}, u32[]{:S(2)}) collective-permute-start(bf16[160,2048]{1,0:T(8,128)(2,1)} %tie.34), channel_id=1, source_target_pairs={{0,16},{8,24},{16,0},{24,8},{1,17},{9,25},{17,1},{25,9},{2,18},{10... | collective-permute-start | bytes 1966088 | tf_op jit(solution)/shard_map/ppermute | solution.py:863
  248.6 33.6 %collective-permute-start.28 = (bf16[160,2048]{1,0:T(8,128)(2,1)}, bf16[160,2048]{1,0:T(8,128)(2,1)}, u32[]{:S(2)}, u32[]{:S(2)}) collective-permute-start(bf16[160,2048]{1,0:T(8,128)(2,1)} %tie.34), channel_id=1, source_target_pairs={{0,8},{8,0},{16,24},{24,16},{1,9},{9,1},{17,25},{25,17},{2,10},{10... | collective-permute-start | bytes 1966088 | tf_op jit(solution)/shard_map/ppermute | solution.py:863
  278.7 174.7 %reduce-scatter.10.cloned.1.call-start = ((), (), s32[]{:S(2)}) async-start(), calls=%async_computation.12 | async-start | bytes 6488064 | tf_op jit(solution)/shard_map/reduce_scatter | solution.py:963
  343.6 154.6 %reduce-scatter.8.cloned.1.call-start = ((), (), s32[]{:S(2)}) async-start(), calls=%async_computation.11 | async-start | bytes 6488064 | tf_op jit(solution)/shard_map/reduce_scatter | solution.py:963
  406.2 34.1 %collective-permute-start.41 = (bf16[320,1024]{1,0:T(8,128)(2,1)}, bf16[320,1024]{1,0:T(8,128)(2,1)}, u32[]{:S(2)}, u32[]{:S(2)}) collective-permute-start(bf16[320,1024]{1,0:T(8,128)(2,1)} %get-tuple-element.121), channel_id=1, source_target_pairs={{0,24},{8,16},{16,8},{24,0},{1,25},{9,17},{17,9},{25,1},{2,26},{10... | collective-permute-start | bytes 1966088 | tf_op jit(solution)/shard_map/ppermute | solution.py:863
  408.8 44.6 %collective-permute-start.43 = (bf16[256,1408]{1,0:T(8,128)(2,1)}, bf16[256,1408]{1,0:T(8,128)(2,1)}, u32[]{:S(2)}, u32[]{:S(2)}) collective-permute-start(bf16[256,1408]{1,0:T(8,128)(2,1)} %reduce-scatter.6.cloned.1.call-done.refs_16_.refs_0_), channel_id=1, source_target_pairs={{0,16},{8,24},{16,0},{24,8},{1,17},{9,25},{17,1},{25,9},{2,18},{10... | collective-permute-start | bytes 2162696 | tf_op jit(solution)/shard_map/ppermute | solution.py:863
  409.3 44.4 %collective-permute-start.42 = (bf16[256,1408]{1,0:T(8,128)(2,1)}, bf16[256,1408]{1,0:T(8,128)(2,1)}, u32[]{:S(2)}, u32[]{:S(2)}) collective-permute-start(bf16[256,1408]{1,0:T(8,128)(2,1)} %reduce-scatter.6.cloned.1.call-done.refs_16_.refs_0_), channel_id=1, source_target_pairs={{0,8},{8,0},{16,24},{24,16},{1,9},{9,1},{17,25},{25,17},{2,10},{10... | collective-permute-start | bytes 2162696 | tf_op jit(solution)/shard_map/ppermute | solution.py:863
  422.4 123.7 %reduce-scatter.12.cloned.1.call-start = ((), (), s32[]{:S(2)}) async-start(), calls=%async_computation.13 | async-start | bytes 2949120 | tf_op jit(solution)/shard_map/reduce_scatter | solution.py:963
  434.8 63.3 %collective-permute-start.44 = (bf16[160,2048]{1,0:T(8,128)(2,1)}, bf16[160,2048]{1,0:T(8,128)(2,1)}, u32[]{:S(2)}, u32[]{:S(2)}) collective-permute-start(bf16[160,2048]{1,0:T(8,128)(2,1)} %get-tuple-element.125), channel_id=1, source_target_pairs={{0,8},{8,0},{16,24},{24,16},{1,9},{9,1},{17,25},{25,17},{2,10},{10... | collective-permute-start | bytes 1966088 | tf_op jit(solution)/shard_map/ppermute | solution.py:863
  437.9 60.2 %collective-permute-start.45 = (bf16[160,2048]{1,0:T(8,128)(2,1)}, bf16[160,2048]{1,0:T(8,128)(2,1)}, u32[]{:S(2)}, u32[]{:S(2)}) collective-permute-start(bf16[160,2048]{1,0:T(8,128)(2,1)} %get-tuple-element.123.rest_0_), channel_id=1, source_target_pairs={{0,16},{8,24},{16,0},{24,8},{1,17},{9,25},{17,1},{25,9},{2,18},{10... | collective-permute-start | bytes 1966088 | tf_op jit(solution)/shard_map/ppermute | solution.py:863
  440.3 57.7 %collective-permute-start.48 = (bf16[256,1408]{1,0:T(8,128)(2,1)}, bf16[256,1408]{1,0:T(8,128)(2,1)}, u32[]{:S(2)}, u32[]{:S(2)}) collective-permute-start(bf16[256,1408]{1,0:T(8,128)(2,1)} %reduce-scatter.6.cloned.1.call-done.refs_16_.refs_0_), channel_id=1, source_target_pairs={{0,24},{8,16},{16,8},{24,0},{1,25},{9,17},{17,9},{25,1},{2,26},{10... | collective-permute-start | bytes 2162696 | tf_op jit(solution)/shard_map/ppermute | solution.py:863
  453.4 44.7 %collective-permute-start.47 = (bf16[176,2048]{1,0:T(8,128)(2,1)}, bf16[176,2048]{1,0:T(8,128)(2,1)}, u32[]{:S(2)}, u32[]{:S(2)}) collective-permute-start(bf16[176,2048]{1,0:T(8,128)(2,1)} %reduce-scatter.10.cloned.1.call-done.refs_1_), channel_id=1, source_target_pairs={{0,16},{8,24},{16,0},{24,8},{1,17},{9,25},{17,1},{25,9},{2,18},{10... | collective-permute-start | bytes 2162696 | tf_op jit(solution)/shard_map/ppermute | solution.py:863
  453.7 44.4 %collective-permute-start.46 = (bf16[176,2048]{1,0:T(8,128)(2,1)}, bf16[176,2048]{1,0:T(8,128)(2,1)}, u32[]{:S(2)}, u32[]{:S(2)}) collective-permute-start(bf16[176,2048]{1,0:T(8,128)(2,1)} %reduce-scatter.10.cloned.1.call-done.refs_1_), channel_id=1, source_target_pairs={{0,8},{8,0},{16,24},{24,16},{1,9},{9,1},{17,25},{25,17},{2,10},{10... | collective-permute-start | bytes 2162696 | tf_op jit(solution)/shard_map/ppermute | solution.py:863
  498.2 120.5 %reduce-scatter.14.cloned.1.call-start = ((), (), s32[]{:S(2)}) async-start(), calls=%async_computation.14 | async-start | bytes 5308416 | tf_op jit(solution)/shard_map/reduce_scatter | solution.py:963
  502.2 43.8 %collective-permute-start.53 = (bf16[176,2048]{1,0:T(8,128)(2,1)S(1)}, bf16[176,2048]{1,0:T(8,128)(2,1)S(1)}, u32[]{:S(2)}, u32[]{:S(2)}) collective-permute-start(bf16[176,2048]{1,0:T(8,128)(2,1)S(1)} %copy-done.19), channel_id=1, source_target_pairs={{0,24},{8,16},{16,8},{24,0},{1,25},{9,17},{17,9},{25,1},{2,26},{10... | collective-permute-start | bytes 2162696 | tf_op jit(solution)/shard_map/ppermute | solution.py:863
  506.5 39.5 %collective-permute-start.51 = (bf16[160,2048]{1,0:T(8,128)(2,1)}, bf16[160,2048]{1,0:T(8,128)(2,1)S(1)}, u32[]{:S(2)}, u32[]{:S(2)}) collective-permute-start(bf16[160,2048]{1,0:T(8,128)(2,1)} %get-tuple-element.129), channel_id=1, source_target_pairs={{0,16},{8,24},{16,0},{24,8},{1,17},{9,25},{17,1},{25,9},{2,18},{10... | collective-permute-start | bytes 1966088 | tf_op jit(solution)/shard_map/ppermute | solution.py:863
  508.0 38.0 %collective-permute-start.50 = (bf16[160,2048]{1,0:T(8,128)(2,1)}, bf16[160,2048]{1,0:T(8,128)(2,1)}, u32[]{:S(2)}, u32[]{:S(2)}) collective-permute-start(bf16[160,2048]{1,0:T(8,128)(2,1)} %get-tuple-element.128.refs_2_), channel_id=1, source_target_pairs={{0,8},{8,0},{16,24},{24,16},{1,9},{9,1},{17,25},{25,17},{2,10},{10... | collective-permute-start | bytes 1966088 | tf_op jit(solution)/shard_map/ppermute | solution.py:863
  597.8 37.1 %collective-permute-start.58 = (bf16[160,2048]{1,0:T(8,128)(2,1)}, bf16[160,2048]{1,0:T(8,128)(2,1)S(1)}, u32[]{:S(2)}, u32[]{:S(2)}) collective-permute-start(bf16[160,2048]{1,0:T(8,128)(2,1)} %get-tuple-element.140.refs_1_), channel_id=1, source_target_pairs={{0,8},{8,0},{16,24},{24,16},{1,9},{9,1},{17,25},{25,17},{2,10},{10... | collective-permute-start | bytes 1966088 | tf_op jit(solution)/shard_map/ppermute | solution.py:863
  (104 other events, 1525.9 us)
Sparse Core Ops, SparseCore 0:
  11.0 32.8 all-gather.7
  46.1 28.5 all-gather.9
  78.0 32.7 all-gather.17
  112.9 59.0 all-gather.11
  173.4 59.0 all-gather.13
  234.1 59.0 all-gather.15
  296.1 63.3 reduce-scatter.5
  362.3 63.2 reduce-scatter.9
  428.5 63.2 reduce-scatter.7
  498.3 36.9 reduce-scatter.11
  561.0 54.7 reduce-scatter.13
where the time goes:
time: 693 us; the launch traced here: 684 us
  Pallas kernels  311 us (45%)
  waiting for transfers between devices  200 us (29%)
  local copies, waits for them, and re-layouts  69.5 us (10%)
  starting transfers between devices  68.7 us (10%)
  other arithmetic  20.2 us (3%)
  between operations  15 us (2%)
    pallas_call x26, Pallas kernels, run(): pl.pallas_call(kernel, grid=grid, out_shape=tuple((shape for shape, _ in...  220 us
    ppermute x64, waiting for transfers between devices, hop(): return lax.ppermute(value, 'dp', [(i, i ^ step) for i in range(4)])  190 us
    ppermute x64, starting transfers between devices, hop(): return lax.ppermute(value, 'dp', [(i, i ^ step) for i in range(4)])  68.1 us
    pallas_call x1, Pallas kernels, attend_back(): pl.pallas_call(functools.partial(attend_back_kernel, rows=rows), grid_spe...  42.7 us
    unnamed x132, local copies, waits for them, and re-layouts  42.5 us
    pallas_call x1, Pallas kernels, attend(): pl.pallas_call(functools.partial(attend_kernel, rows=rows), grid_spec=plt...  29.2 us
  transfers between devices with their start and end apart: 78, of which 24 were waited for; matrix products, arithmetic and copies ran while one was open for 9% of the time, Pallas kernels for 43%

commit v1 on v0

--- a/solution.py
+++ b/solution.py
@@ -52,7 +52,7 @@
     "middle_back": 200,
     "down_product": 4,
     "output_gradient": 2,
-    "project_back": 2,
+    "project_back": 50,
     "sum_output": 100,
     "sum_tokens": 100,
     "spread_up": 300,
@@ -1080,20 +1080,25 @@
     out_raw = output_gradient_of(mixed_all, d_heads, wide, (first,))
     downs_far = hop(tie(down_part, dkv), 3)
     own_dkv = tie(own_dkv, out_raw, *terms[1:], downs_far)
+    gate_part = tie(gate_part, own_dkv)
+    gates_one, gates_two = hop(gate_part, 1), hop(gate_part, 2)
     both_raw, *fs = project_back(
         dq, own_dkv, cos_t, sin_t, w_qkv, rows, hat, out_raw
     )
+    fs[5], fs[6] = (tie(f, gates_one, gates_two) for f in fs[5:])
     both_part = far(both_raw)
     layer_output = sum_output(terms, middle, (fs[6],))
     came = (*reduce_first(fs), *reduce_plain(fs))
     first, terms = reduce_second(fs, came, came[2:])
-    gates = gather_plane(tie(gate_part, first), (both_part,))
+    half_rows = gate_part.shape[0] // 2
+    gates_one, gates_two = tie(gates_one, first), tie(gates_two, first)
+    gates_far = [hop(gates_two[:half_rows], 1), hop(gates_one[half_rows:], 2)]
     token_gradient = sum_tokens(terms, tokens, d_middle)
 
     gate_gradient, gain_g = spread_columns(
         "spread_gate",
         mine[None],
-        jnp.stack([*gates[:3], join(gates[3:])]),
+        jnp.stack([gate_part, gates_one, gates_two, join(gates_far)]),
         gain_f,
         gate_weight,
         shards,

time: 693 us -> 684 us (0.987)
  the two profiles are of different devices: /device:TPU:28 before, /device:TPU:17 now
where the time goes in v1:
time: 684 us; the launch traced here: 674 us
  Pallas kernels  344 us (50%)
  waiting for transfers between devices  171 us (25%)
  local copies, waits for them, and re-layouts  67.4 us (10%)
  starting transfers between devices  57 us (8%)
  other arithmetic  19.9 us (3%)
  between operations  14.9 us (2%)
    pallas_call x26, Pallas kernels, run(): pl.pallas_call(kernel, grid=grid, out_shape=tuple((shape for shape, _ in...  220 us
    ppermute x64, waiting for transfers between devices, hop(): return lax.ppermute(value, 'dp', [(i, i ^ step) for i in range(4)])  162 us
    pallas_call x1, Pallas kernels, attend_back(): pl.pallas_call(functools.partial(attend_back_kernel, rows=rows), grid_spe...  62.1 us
    ppermute x64, starting transfers between devices, hop(): return lax.ppermute(value, 'dp', [(i, i ^ step) for i in range(4)])  53.9 us
    pallas_call x1, Pallas kernels, attend(): pl.pallas_call(functools.partial(attend_kernel, rows=rows), grid_spec=plt...  43.3 us
    unnamed x130, local copies, waits for them, and re-layouts  41.2 us
  transfers between devices with their start and end apart: 78, of which 25 were waited for; matrix products, arithmetic and copies ran while one was open for 9% of the time, Pallas kernels for 50%

profile of v1, /device:TPU:17, one launch (start us, length us, event | category | flops | bytes accessed | tf_op | source)
XLA Modules:
  0.0 674.3 jit_solution(9184701759120079519)
XLA Ops:
  17.8 24.1 %collective-permute-done.1 = s32[1,2]{1,0:T(1,128)S(1)} collective-permute-done((s32[1,2]{1,0:T(1,128)}, s32[1,2]{1,0:T(1,128)S(1)}, u32[]{:S(2)}, u32[]{:S(2)}) %collective-permute-start.1) | collective-permute-done | bytes 40 | tf_op jit(solution)/shard_map/ppermute | solution.py:863
  88.5 22.1 %collective-permute-done.8.rest_1_.refs_2_.refs_9_.refs_12_ = bf16[1024,512]{1,0:T(8,128)(2,1)S(1)} collective-permute-done((bf16[1024,512]{1,0:T(8,128)(2,1)}, bf16[1024,512]{1,0:T(8,128)(2,1)S(1)}, u32[]{:S(2)}, u32[]{:S(2)}) %collective-permute-start.8) | collective-permute-done | bytes 1048608 | tf_op jit(solution)/shard_map/ppermute | solution.py:863
  124.4 43.3 %attend.1 = (bf16[1280,512]{1,0:T(8,128)(2,1)}, f32[4,1,2560]{2,1,0:T(1,128)}) custom-call(s32[9]{0:T(128)} %pad_add_fusion.3.where, bf16[1280,512]{1,0:T(8,128)(2,1)} %get-tuple-element.91.q_ref, bf16[8,1280,128]{2,1,0:T(8,128)(2,1)} %bitcast.23, s32[4,2,2560]{2,1,0:T(2,128)} %concatenate.38.bound_ref, bf16[1024,512]{1,0:T(8,128)(2,1)} %copy-done.8, ...), custom_call_target="tpu_custom_call" | custom-call | flops 320000000000 | bytes 1000000000 | tf_op jit(solution)/shard_map/attend/pallas_call | solution.py:326
  180.1 7.6 %collective-permute-done.16.refs_3_ = bf16[320,512]{1,0:T(8,128)(2,1)S(1)} collective-permute-done((bf16[320,512]{1,0:T(8,128)(2,1)S(1)}, bf16[320,512]{1,0:T(8,128)(2,1)S(1)}, u32[]{:S(2)}, u32[]{:S(2)}) %collective-permute-start.16) | collective-permute-done | bytes 327712 | tf_op jit(solution)/shard_map/ppermute | solution.py:863
  190.1 9.8 %output_product.1 = (bf16[160,2048]{1,0:T(8,128)(2,1)}, bf16[160,2048]{1,0:T(8,128)(2,1)}, f32[320,2048]{1,0:T(8,128)}, bf16[160,2048]{1,0:T(8,128)(2,1)}, bf16[160,2048]{1,0:T(8,128)(2,1)}) custom-call(s32[3]{0:T(128)} %pad_add_fusion.2.refs_0_, bf16[320,512]{1,0:T(8,128)(2,1)} %get-tuple-element.164.refs_1_, bf16[320,512]{1,0:T(8,128)(2,1)} %copy-done.18, ...), custom_call_target="tpu_custom_call" | custom-call | flops 2400000000 | bytes 7500000 | tf_op jit(solution)/shard_map/output_product/pallas_call | solution.py:97
  215.7 13.0 %hidden_back.1.refs_1_.refs_9_.refs_3_ = bf16[1280,1408]{1,0:T(8,128)(2,1)} custom-call(bf16[1280,2048]{1,0:T(8,128)(2,1)} %constant_dynamic-update-slice_fusion.refs_0_.refs_1_, bf16[1408,2048]{1,0:T(8,128)(2,1)} %all-gather.12.cloned.1.call-done.refs_1_, bf16[160,2048]{1,0:T(8,128)(2,1)} %get-tuple-element.95.refs_2_.refs_1_), custom_call_target="tpu_custom_call" | custom-call | flops 3200000000 | bytes 10000000 | tf_op jit(solution)/shard_map/hidden_back/pallas_call | solution.py:97
  236.9 11.9 %collective-permute-done.26.refs_7_.refs_2_ = bf16[160,2048]{1,0:T(8,128)(2,1)S(1)} collective-permute-done((bf16[160,2048]{1,0:T(8,128)(2,1)}, bf16[160,2048]{1,0:T(8,128)(2,1)S(1)}, u32[]{:S(2)}, u32[]{:S(2)}) %collective-permute-start.26) | collective-permute-done | bytes 655392 | tf_op jit(solution)/shard_map/ppermute | solution.py:863
  254.9 15.8 %gate_product.1 = (bf16[1280,1408]{1,0:T(8,128)(2,1)}, bf16[1280,1408]{1,0:T(8,128)(2,1)}, bf16[1280,2048]{1,0:T(8,128)(2,1)}) custom-call(bf16[160,2048]{1,0:T(8,128)(2,1)} %get-tuple-element.94.refs_1_.refs_0_, bf16[160,2048]{1,0:T(8,128)(2,1)} %get-tuple-element.95.refs_2_.refs_1_, bf16[160,2048]{1,0:T(8,128)(2,1)} %copy-done.10, ...), custom_call_target="tpu_custom_call" | custom-call | flops 1600000000 | bytes 5000000 | tf_op jit(solution)/shard_map/gate_product/pallas_call | solution.py:97
  270.7 12.9 %up_gradient.1.refs_4_ = bf16[2048,1408]{1,0:T(8,128)(2,1)} custom-call(bf16[1280,2048]{1,0:T(8,128)(2,1)} %get-tuple-element.97.refs_0_, bf16[1280,1408]{1,0:T(8,128)(2,1)} %get-tuple-element.100.refs_1_.refs_2_.refs_3_), custom_call_target="tpu_custom_call" | custom-call | flops 1600000000 | bytes 5000000 | tf_op jit(solution)/shard_map/up_gradient/pallas_call | solution.py:97
  287.9 6.9 %all-gather.16.cloned.1.call-done.refs_1_.refs_3_.refs_5_ = bf16[2048,1408]{1,0:T(8,128)(2,1)} async-done(((bf16[256,1408]{1,0:T(8,128)(2,1)}), bf16[2048,1408]{1,0:T(8,128)(2,1)}) %all-gather.16.cloned.1.call-update) | async-done | bytes 5767184 | tf_op jit(solution)/shard_map/all_gather | solution.py:962
  294.8 7.0 %up_product.2 = (bf16[1280,1408]{1,0:T(8,128)(2,1)}, bf16[1280,1408]{1,0:T(8,128)(2,1)}) custom-call(bf16[1280,2048]{1,0:T(8,128)(2,1)} %get-tuple-element.97.refs_0_, bf16[2048,1408]{1,0:T(8,128)(2,1)} %all-gather.16.cloned.1.call-done.refs_1_.refs_3_.refs_5_, bf16[1280,1408]{1,0:T(8,128)(2,1)} %get-tuple-element.99.refs_2_, ...), custom_call_target="tpu_custom_call" | custom-call | flops 80000000000 | bytes 250000000 | tf_op jit(solution)/shard_map/up_product/pallas_call | solution.py:97
  310.0 8.9 %back_first.1 = (bf16[160,2048]{1,0:T(8,128)(2,1)}, bf16[160,2048]{1,0:T(8,128)(2,1)}) custom-call(bf16[1280,1408]{1,0:T(8,128)(2,1)} %get-tuple-element.104.refs_0_.refs_5_, bf16[1280,1408]{1,0:T(8,128)(2,1)} %get-tuple-element.100.refs_1_.refs_2_.refs_3_, bf16[2048,1408]{1,0:T(8,128)(2,1)} %all-gather.14.cloned.1.call-done.refs_8_.refs_2_.refs_4_, ...), custom_call_target="tpu_custom_call" | custom-call | flops 3200000000 | bytes 10000000 | tf_op jit(solution)/shard_map/back_first/pallas_call | solution.py:97
  321.2 12.4 %up_product.3 = (bf16[1280,1408]{1,0:T(8,128)(2,1)}, bf16[1280,1408]{1,0:T(8,128)(2,1)}) custom-call(bf16[1280,2048]{1,0:T(8,128)(2,1)} %get-tuple-element.97.refs_0_, bf16[2048,1408]{1,0:T(8,128)(2,1)} %all-gather.16.cloned.1.call-done.refs_1_.refs_3_.refs_5_, ...), custom_call_target="tpu_custom_call", output_to_operand_aliasing={{0}: (4, {}), {1}: (5, {})} | custom-call | flops 80000000000 | bytes 250000000 | tf_op jit(solution)/shard_map/up_product/pallas_call | solution.py:97
  333.7 11.9 %down_gradient.1.refs_6_ = bf16[1408,2048]{1,0:T(8,128)(2,1)} custom-call(bf16[1280,1408]{1,0:T(8,128)(2,1)} %get-tuple-element.106.refs_0_, bf16[1280,2048]{1,0:T(8,128)(2,1)} %constant_dynamic-update-slice_fusion.refs_0_.refs_1_), custom_call_target="tpu_custom_call" | custom-call | flops 160000000 | bytes 500000 | tf_op jit(solution)/shard_map/down_gradient/pallas_call | solution.py:97
  346.7 12.8 %back_product.2 = (bf16[160,2048]{1,0:T(8,128)(2,1)}, bf16[160,2048]{1,0:T(8,128)(2,1)}, bf16[160,2048]{1,0:T(8,128)(2,1)}, bf16[160,2048]{1,0:T(8,128)(2,1)}) custom-call(bf16[1280,1408]{1,0:T(8,128)(2,1)} %get-tuple-element.107.refs_0_.refs_1_, bf16[1280,1408]{1,0:T(8,128)(2,1)} %get-tuple-element.107.refs_0_.refs_1_, ...), custom_call_target="tpu_custom_call" | custom-call | flops 3200000000 | bytes 10000000 | tf_op jit(solution)/shard_map/back_product/pallas_call | solution.py:97
  367.5 8.9 %back_product.3.refs_1_ = bf16[320,2048]{1,0:T(8,128)(2,1)} custom-call(bf16[1280,1408]{1,0:T(8,128)(2,1)} %get-tuple-element.107.refs_0_.refs_1_, bf16[1280,1408]{1,0:T(8,128)(2,1)} %get-tuple-element.100.refs_1_.refs_2_.refs_3_, bf16[2048,1408]{1,0:T(8,128)(2,1)} %all-gather.14.cloned.1.call-done.refs_8_.refs_2_.refs_4_, ...), custom_call_target="tpu_custom_call" | custom-call | flops 3200000000 | bytes 10000000 | tf_op jit(solution)/shard_map/back_product/pallas_call | solution.py:97
  378.4 14.0 %collective-permute-done.35.refs_2_ = bf16[160,2048]{1,0:T(8,128)(2,1)S(1)} collective-permute-done((bf16[160,2048]{1,0:T(8,128)(2,1)S(1)}, bf16[160,2048]{1,0:T(8,128)(2,1)S(1)}, u32[]{:S(2)}, u32[]{:S(2)}) %collective-permute-start.35) | collective-permute-done | bytes 655392 | tf_op jit(solution)/shard_map/ppermute | solution.py:863
  393.2 12.1 %middle_back.1 = (f32[320,2048]{1,0:T(8,128)}, bf16[320,1024]{1,0:T(8,128)(2,1)}, bf16[320,1024]{1,0:T(8,128)(2,1)}, bf16[320,1024]{1,0:T(8,128)(2,1)}, bf16[320,1024]{1,0:T(8,128)(2,1)}) custom-call(s32[3]{0:T(128)} %pad_add_fusion.2.refs_0_, bf16[320,2048]{1,0:T(8,128)(2,1)} %back_product.3.refs_1_, bf16[160,2048]{1,0:T(8,128)(2,1)} %copy-done.50, ...), custom_call_target="tpu_custom_call" | custom-call | flops 160000000000 | bytes 500000000 | tf_op jit(solution)/shard_map/middle_back/pallas_call | solution.py:97
  409.3 12.6 %gate_gradient.1.refs_2_ = bf16[2048,1408]{1,0:T(8,128)(2,1)} custom-call(bf16[1280,2048]{1,0:T(8,128)(2,1)} %get-tuple-element.97.refs_0_, bf16[1280,1408]{1,0:T(8,128)(2,1)} %get-tuple-element.107.refs_0_.refs_1_, bf16[320,1024]{1,0:T(8,128)(2,1)} %get-tuple-element.116.refs_2_), custom_call_target="tpu_custom_call" | custom-call | flops 1600000000 | bytes 5000000 | tf_op jit(solution)/shard_map/gate_gradient/pallas_call | solution.py:97
  422.0 12.4 %down_product.1 = (bf16[320,2048]{1,0:T(8,128)(2,1)}, bf16[160,2048]{1,0:T(8,128)(2,1)}, bf16[160,2048]{1,0:T(8,128)(2,1)}, bf16[160,2048]{1,0:T(8,128)(2,1)}, b...) custom-call(bf16[1280,1408]{1,0:T(8,128)(2,1)} %get-tuple-element.106.refs_0_, ...), custom_call_target="tpu_custom_call" | custom-call | flops 3200000000 | bytes 10000000 | tf_op jit(solution)/shard_map/down_product/pallas_call | solution.py:97
  440.7 8.7 %collective-permute-done.43.rest_2_ = bf16[256,1408]{1,0:T(8,128)(2,1)} collective-permute-done((bf16[256,1408]{1,0:T(8,128)(2,1)}, bf16[256,1408]{1,0:T(8,128)(2,1)}, u32[]{:S(2)}, u32[]{:S(2)}) %collective-permute-start.43) | collective-permute-done | bytes 720928 | tf_op jit(solution)/shard_map/ppermute | solution.py:863
  451.8 62.1 %attend_back.1 = (bf16[1280,512]{1,0:T(8,128)(2,1)}, bf16[8,1280,128]{2,1,0:T(8,128)(2,1)}) custom-call(s32[9]{0:T(128)} %pad_add_fusion.3.where, bf16[1280,512]{1,0:T(8,128)(2,1)} %get-tuple-element.91.q_ref, bf16[8,1280,128]{2,1,0:T(8,128)(2,1)} %bitcast.24, s32[4,2,2560]{2,1,0:T(2,128)} %concatenate.38.bound_ref, bf16[1280,1024]{1,0:T(8,128)(2,1)} %copy-done.15, ...), custom_call_target="tpu_custom_call" | custom-call | flops 799999983616 | bytes 2500000000 | tf_op jit(solution)/shard_map/attend_back/pallas_call | solution.py:432
  522.5 7.1 %output_gradient.1.refs_1_.refs_6_ = bf16[2048,512]{1,0:T(8,128)(2,1)} custom-call(bf16[1280,2048]{1,0:T(8,128)(2,1)} %constant_dynamic-update-slice_fusion.5.refs_17_.refs_0_, bf16[1280,1024]{1,0:T(8,128)(2,1)} %copy-done.15, bf16[160,2048]{1,0:T(8,128)(2,1)} %get-tuple-element.128.refs_2_), custom_call_target="tpu_custom_call" | custom-call | flops 1600000000 | bytes 5000000 | tf_op jit(solution)/shard_map/output_gradient/pallas_call | solution.py:97
  533.0 15.6 %collective-permute-done.52.refs_5_.refs_4_ = bf16[160,2048]{1,0:T(8,128)(2,1)S(1)} collective-permute-done((bf16[160,2048]{1,0:T(8,128)(2,1)}, bf16[160,2048]{1,0:T(8,128)(2,1)S(1)}, u32[]{:S(2)}, u32[]{:S(2)}) %collective-permute-start.52) | collective-permute-done | bytes 655392 | tf_op jit(solution)/shard_map/ppermute | solution.py:863
  548.6 9.5 %collective-permute-done.51.refs_4_.refs_3_ = bf16[160,2048]{1,0:T(8,128)(2,1)S(1)} collective-permute-done((bf16[160,2048]{1,0:T(8,128)(2,1)}, bf16[160,2048]{1,0:T(8,128)(2,1)S(1)}, u32[]{:S(2)}, u32[]{:S(2)}) %collective-permute-start.51) | collective-permute-done | bytes 655392 | tf_op jit(solution)/shard_map/ppermute | solution.py:863
  561.5 13.7 %project_back.1 = (bf16[2048,1152]{1,0:T(8,128)(2,1)}, bf16[320,2048]{1,0:T(8,128)(2,1)}, bf16[160,2048]{1,0:T(8,128)(2,1)}, bf16[160,2048]{1,0:T(8,128)(2,1)}, ...) custom-call(bf16[1280,512]{1,0:T(8,128)(2,1)} %get-tuple-element.131, ...), custom_call_target="tpu_custom_call" | custom-call | flops 40000000000 | bytes 125000000 | tf_op jit(solution)/shard_map/project_back/pallas_call | solution.py:97
  582.5 6.8 %spread_up.1 = (f32[256,5632]{1,0:T(8,128)}, f32[256,1]{1,0:T(8,128)}) custom-call(s32[1]{0:T(128)} %bitcast.which.refs_0_, bf16[4,256,1408]{2,1,0:T(8,128)(2,1)} %pad_maximum_fusion.1.grads, f32[256,1]{1,0:T(8,128)} %copy.69.gain, bf16[256,5632]{1,0:T(8,128)(2,1)} %weight.3), custom_call_target="tpu_custom_call" | custom-call | flops 240000008192 | bytes 750000000 | tf_op jit(solution)/shard_map/spread_up/pallas_call | solution.py:174
  594.0 10.0 %collective-permute-done.58.refs_3_ = bf16[160,2048]{1,0:T(8,128)(2,1)} collective-permute-done((bf16[160,2048]{1,0:T(8,128)(2,1)}, bf16[160,2048]{1,0:T(8,128)(2,1)}, u32[]{:S(2)}, u32[]{:S(2)}) %collective-permute-start.58) | collective-permute-done | bytes 655392 | tf_op jit(solution)/shard_map/ppermute | solution.py:863
  622.4 6.9 %spread_gate.1 = (f32[256,5632]{1,0:T(8,128)}, f32[256,1]{1,0:T(8,128)}) custom-call(s32[1]{0:T(128)} %bitcast.which.refs_0_, bf16[4,256,1408]{2,1,0:T(8,128)(2,1)} %pad_maximum_fusion.grads, f32[256,1]{1,0:T(8,128)} %copy.69.gain, bf16[256,5632]{1,0:T(8,128)(2,1)} %weight.2), custom_call_target="tpu_custom_call" | custom-call | flops 80000000 | bytes 250000 | tf_op jit(solution)/shard_map/spread_gate/pallas_call | solution.py:174
  633.9 6.5 sum_tokens.1
  640.4 6.6 collective-permute-done.64.refs_4_
  647.1 12.1 %collective-permute-done.63.refs_3_ = bf16[256,1152]{1,0:T(8,128)(2,1)S(1)} collective-permute-done((bf16[256,1152]{1,0:T(8,128)(2,1)}, bf16[256,1152]{1,0:T(8,128)(2,1)S(1)}, u32[]{:S(2)}, u32[]{:S(2)}) %collective-permute-start.63) | collective-permute-done | bytes 589856 | tf_op jit(solution)/shard_map/ppermute | solution.py:863
  (368 shorter events, 213.6 us)
Async XLA Ops:
  7.2 38.2 %all-gather.8.cloned.1.call-start = ((), (), s32[]{:S(2)}) async-start(), calls=%async_computation.5 | async-start | bytes 2949120 | tf_op jit(solution)/shard_map/all_gather | solution.py:962
  10.9 65.6 %all-gather.10.cloned.1.call-start = ((), (), s32[]{:S(2)}) async-start(), calls=%async_computation.6 | async-start | bytes 2359296 | tf_op jit(solution)/shard_map/all_gather | solution.py:962
  11.0 32.2 %collective-permute-start.5 = (bf16[320,2048]{1,0:T(8,128)(2,1)}, bf16[320,2048]{1,0:T(8,128)(2,1)}, u32[]{:S(2)}, u32[]{:S(2)}) collective-permute-start(bf16[320,2048]{1,0:T(8,128)(2,1)} %refs_5_.1), channel_id=1, source_target_pairs={{0,8},{8,0},{16,24},{24,16},{1,9},{9,1},{17,25},{25,17},{2,10},{10... | collective-permute-start | bytes 3932168 | tf_op jit(solution)/shard_map/ppermute | solution.py:863
  45.5 78.9 %all-gather.18.cloned.1.call-start = ((), (), s32[]{:S(2)}) async-start(), calls=%async_computation.15 | async-start | bytes 2949120 | tf_op jit(solution)/shard_map/all_gather | solution.py:1015
  79.6 136.1 %all-gather.12.cloned.1.call-start = ((), (), s32[]{:S(2)}) async-start(), calls=%async_computation.7 | async-start | bytes 6488064 | tf_op jit(solution)/shard_map/all_gather | solution.py:962
  80.6 174.4 %all-gather.14.cloned.1.call-start = ((), (), s32[]{:S(2)}) async-start(), calls=%async_computation.8 | async-start | bytes 6488064 | tf_op jit(solution)/shard_map/all_gather | solution.py:962
  86.4 208.4 %all-gather.16.cloned.1.call-start = ((), (), s32[]{:S(2)}) async-start(), calls=%async_computation.9 | async-start | bytes 6488064 | tf_op jit(solution)/shard_map/all_gather | solution.py:962
  113.3 279.1 %reduce-scatter.6.cloned.1.call-start = ((), (), s32[]{:S(2)}) async-start(), calls=%async_computation.10 | async-start | bytes 6488064 | tf_op jit(solution)/shard_map/reduce_scatter | solution.py:963
  117.7 50.0 %collective-permute-start.14 = (bf16[320,2048]{1,0:T(8,128)(2,1)}, bf16[320,2048]{1,0:T(8,128)(2,1)}, u32[]{:S(2)}, u32[]{:S(2)}) collective-permute-start(bf16[320,2048]{1,0:T(8,128)(2,1)} %tie.27.refs_0_), channel_id=1, source_target_pairs={{0,16},{8,24},{16,0},{24,8},{1,17},{9,25},{17,1},{25,9},{2,18},{10... | collective-permute-start | bytes 3932168 | tf_op jit(solution)/shard_map/ppermute | solution.py:863
  118.1 49.5 %collective-permute-start.13 = (bf16[320,2048]{1,0:T(8,128)(2,1)}, bf16[320,2048]{1,0:T(8,128)(2,1)}, u32[]{:S(2)}, u32[]{:S(2)}) collective-permute-start(bf16[320,2048]{1,0:T(8,128)(2,1)} %tie.27.refs_0_), channel_id=1, source_target_pairs={{0,8},{8,0},{16,24},{24,16},{1,9},{9,1},{17,25},{25,17},{2,10},{10... | collective-permute-start | bytes 3932168 | tf_op jit(solution)/shard_map/ppermute | solution.py:863
  121.0 46.7 %collective-permute-start.11 = (bf16[512,512]{1,0:T(8,128)(2,1)}, bf16[512,512]{1,0:T(8,128)(2,1)}, u32[]{:S(2)}, u32[]{:S(2)}) collective-permute-start(bf16[512,512]{1,0:T(8,128)(2,1)} %slice.60), channel_id=1, source_target_pairs={{0,8},{8,0},{16,24},{24,16},{1,9},{9,1},{17,25},{25,17},{2,10},{10... | collective-permute-start | bytes 1572872 | tf_op jit(solution)/shard_map/ppermute | solution.py:863
  123.4 44.3 %collective-permute-start.12 = (bf16[512,512]{1,0:T(8,128)(2,1)}, bf16[512,512]{1,0:T(8,128)(2,1)}, u32[]{:S(2)}, u32[]{:S(2)}) collective-permute-start(bf16[512,512]{1,0:T(8,128)(2,1)} %slice.61), channel_id=1, source_target_pairs={{0,16},{8,24},{16,0},{24,8},{1,17},{9,25},{17,1},{25,9},{2,18},{10... | collective-permute-start | bytes 1572872 | tf_op jit(solution)/shard_map/ppermute | solution.py:863
  201.0 34.7 %collective-permute-start.24 = (bf16[160,2048]{1,0:T(8,128)(2,1)S(1)}, bf16[160,2048]{1,0:T(8,128)(2,1)S(1)}, u32[]{:S(2)}, u32[]{:S(2)}) collective-permute-start(bf16[160,2048]{1,0:T(8,128)(2,1)S(1)} %copy-done.30), channel_id=1, source_target_pairs={{0,16},{8,24},{16,0},{24,8},{1,17},{9,25},{17,1},{25,9},{2,18},{10... | collective-permute-start | bytes 1966088 | tf_op jit(solution)/shard_map/ppermute | solution.py:863
  252.0 34.5 %collective-permute-start.29 = (bf16[160,2048]{1,0:T(8,128)(2,1)}, bf16[160,2048]{1,0:T(8,128)(2,1)S(1)}, u32[]{:S(2)}, u32[]{:S(2)}) collective-permute-start(bf16[160,2048]{1,0:T(8,128)(2,1)} %tie.35), channel_id=1, source_target_pairs={{0,16},{8,24},{16,0},{24,8},{1,17},{9,25},{17,1},{25,9},{2,18},{10... | collective-permute-start | bytes 1966088 | tf_op jit(solution)/shard_map/ppermute | solution.py:863
  252.0 42.8 %collective-permute-start.27 = (bf16[160,2048]{1,0:T(8,128)(2,1)}, bf16[160,2048]{1,0:T(8,128)(2,1)}, u32[]{:S(2)}, u32[]{:S(2)}) collective-permute-start(bf16[160,2048]{1,0:T(8,128)(2,1)} %tie.35), channel_id=1, source_target_pairs={{0,8},{8,0},{16,24},{24,16},{1,9},{9,1},{17,25},{25,17},{2,10},{10... | collective-permute-start | bytes 1966088 | tf_op jit(solution)/shard_map/ppermute | solution.py:863
  253.3 41.5 %collective-permute-start.30 = (bf16[160,2048]{1,0:T(8,128)(2,1)}, bf16[160,2048]{1,0:T(8,128)(2,1)}, u32[]{:S(2)}, u32[]{:S(2)}) collective-permute-start(bf16[160,2048]{1,0:T(8,128)(2,1)} %tie.36), channel_id=1, source_target_pairs={{0,16},{8,24},{16,0},{24,8},{1,17},{9,25},{17,1},{25,9},{2,18},{10... | collective-permute-start | bytes 1966088 | tf_op jit(solution)/shard_map/ppermute | solution.py:863
  253.9 33.1 %collective-permute-start.28 = (bf16[160,2048]{1,0:T(8,128)(2,1)}, bf16[160,2048]{1,0:T(8,128)(2,1)}, u32[]{:S(2)}, u32[]{:S(2)}) collective-permute-start(bf16[160,2048]{1,0:T(8,128)(2,1)} %tie.36), channel_id=1, source_target_pairs={{0,8},{8,0},{16,24},{24,16},{1,9},{9,1},{17,25},{25,17},{2,10},{10... | collective-permute-start | bytes 1966088 | tf_op jit(solution)/shard_map/ppermute | solution.py:863
  283.7 165.7 %reduce-scatter.10.cloned.1.call-start = ((), (), s32[]{:S(2)}) async-start(), calls=%async_computation.12 | async-start | bytes 6488064 | tf_op jit(solution)/shard_map/reduce_scatter | solution.py:963
  345.6 168.3 %reduce-scatter.8.cloned.1.call-start = ((), (), s32[]{:S(2)}) async-start(), calls=%async_computation.11 | async-start | bytes 6488064 | tf_op jit(solution)/shard_map/reduce_scatter | solution.py:963
  407.9 41.5 %collective-permute-start.43 = (bf16[256,1408]{1,0:T(8,128)(2,1)}, bf16[256,1408]{1,0:T(8,128)(2,1)}, u32[]{:S(2)}, u32[]{:S(2)}) collective-permute-start(bf16[256,1408]{1,0:T(8,128)(2,1)} %reduce-scatter.6.cloned.1.call-done.refs_16_.refs_0_), channel_id=1, source_target_pairs={{0,16},{8,24},{16,0},{24,8},{1,17},{9,25},{17,1},{25,9},{2,18},{10... | collective-permute-start | bytes 2162696 | tf_op jit(solution)/shard_map/ppermute | solution.py:863
  409.2 41.3 %collective-permute-start.42 = (bf16[256,1408]{1,0:T(8,128)(2,1)}, bf16[256,1408]{1,0:T(8,128)(2,1)}, u32[]{:S(2)}, u32[]{:S(2)}) collective-permute-start(bf16[256,1408]{1,0:T(8,128)(2,1)} %reduce-scatter.6.cloned.1.call-done.refs_16_.refs_0_), channel_id=1, source_target_pairs={{0,8},{8,0},{16,24},{24,16},{1,9},{9,1},{17,25},{25,17},{2,10},{10... | collective-permute-start | bytes 2162696 | tf_op jit(solution)/shard_map/ppermute | solution.py:863
  422.0 136.2 %reduce-scatter.12.cloned.1.call-start = ((), (), s32[]{:S(2)}) async-start(), calls=%async_computation.13 | async-start | bytes 2949120 | tf_op jit(solution)/shard_map/reduce_scatter | solution.py:963
  434.4 79.4 %collective-permute-start.44 = (bf16[160,2048]{1,0:T(8,128)(2,1)}, bf16[160,2048]{1,0:T(8,128)(2,1)}, u32[]{:S(2)}, u32[]{:S(2)}) collective-permute-start(bf16[160,2048]{1,0:T(8,128)(2,1)} %get-tuple-element.125), channel_id=1, source_target_pairs={{0,8},{8,0},{16,24},{24,16},{1,9},{9,1},{17,25},{25,17},{2,10},{10... | collective-permute-start | bytes 1966088 | tf_op jit(solution)/shard_map/ppermute | solution.py:863
  437.0 76.8 %collective-permute-start.45 = (bf16[160,2048]{1,0:T(8,128)(2,1)}, bf16[160,2048]{1,0:T(8,128)(2,1)}, u32[]{:S(2)}, u32[]{:S(2)}) collective-permute-start(bf16[160,2048]{1,0:T(8,128)(2,1)} %get-tuple-element.123.rest_0_), channel_id=1, source_target_pairs={{0,16},{8,24},{16,0},{24,8},{1,17},{9,25},{17,1},{25,9},{2,18},{10... | collective-permute-start | bytes 1966088 | tf_op jit(solution)/shard_map/ppermute | solution.py:863
  438.4 75.5 %collective-permute-start.48 = (bf16[256,1408]{1,0:T(8,128)(2,1)}, bf16[256,1408]{1,0:T(8,128)(2,1)}, u32[]{:S(2)}, u32[]{:S(2)}) collective-permute-start(bf16[256,1408]{1,0:T(8,128)(2,1)} %reduce-scatter.6.cloned.1.call-done.refs_16_.refs_0_), channel_id=1, source_target_pairs={{0,24},{8,16},{16,8},{24,0},{1,25},{9,17},{17,9},{25,1},{2,26},{10... | collective-permute-start | bytes 2162696 | tf_op jit(solution)/shard_map/ppermute | solution.py:863
  449.4 64.4 %collective-permute-start.47 = (bf16[176,2048]{1,0:T(8,128)(2,1)}, bf16[176,2048]{1,0:T(8,128)(2,1)}, u32[]{:S(2)}, u32[]{:S(2)}) collective-permute-start(bf16[176,2048]{1,0:T(8,128)(2,1)} %reduce-scatter.10.cloned.1.call-done.refs_1_), channel_id=1, source_target_pairs={{0,16},{8,24},{16,0},{24,8},{1,17},{9,25},{17,1},{25,9},{2,18},{10... | collective-permute-start | bytes 2162696 | tf_op jit(solution)/shard_map/ppermute | solution.py:863
  450.5 63.4 %collective-permute-start.46 = (bf16[176,2048]{1,0:T(8,128)(2,1)}, bf16[176,2048]{1,0:T(8,128)(2,1)}, u32[]{:S(2)}, u32[]{:S(2)}) collective-permute-start(bf16[176,2048]{1,0:T(8,128)(2,1)} %reduce-scatter.10.cloned.1.call-done.refs_1_), channel_id=1, source_target_pairs={{0,8},{8,0},{16,24},{24,16},{1,9},{9,1},{17,25},{25,17},{2,10},{10... | collective-permute-start | bytes 2162696 | tf_op jit(solution)/shard_map/ppermute | solution.py:863
  513.9 116.9 %reduce-scatter.14.cloned.1.call-start = ((), (), s32[]{:S(2)}) async-start(), calls=%async_computation.14 | async-start | bytes 5308416 | tf_op jit(solution)/shard_map/reduce_scatter | solution.py:963
  516.0 32.6 %collective-permute-start.52 = (bf16[160,2048]{1,0:T(8,128)(2,1)}, bf16[160,2048]{1,0:T(8,128)(2,1)S(1)}, u32[]{:S(2)}, u32[]{:S(2)}) collective-permute-start(bf16[160,2048]{1,0:T(8,128)(2,1)} %tie.39), channel_id=1, source_target_pairs={{0,16},{8,24},{16,0},{24,8},{1,17},{9,25},{17,1},{25,9},{2,18},{10... | collective-permute-start | bytes 1966088 | tf_op jit(solution)/shard_map/ppermute | solution.py:863
  517.0 41.1 %collective-permute-start.53 = (bf16[176,2048]{1,0:T(8,128)(2,1)S(1)}, bf16[176,2048]{1,0:T(8,128)(2,1)S(1)}, u32[]{:S(2)}, u32[]{:S(2)}) collective-permute-start(bf16[176,2048]{1,0:T(8,128)(2,1)S(1)} %copy-done.19), channel_id=1, source_target_pairs={{0,24},{8,16},{16,8},{24,0},{1,25},{9,17},{17,9},{25,1},{2,26},{10... | collective-permute-start | bytes 2162696 | tf_op jit(solution)/shard_map/ppermute | solution.py:863
  521.4 36.7 %collective-permute-start.51 = (bf16[160,2048]{1,0:T(8,128)(2,1)}, bf16[160,2048]{1,0:T(8,128)(2,1)S(1)}, u32[]{:S(2)}, u32[]{:S(2)}) collective-permute-start(bf16[160,2048]{1,0:T(8,128)(2,1)} %get-tuple-element.129), channel_id=1, source_target_pairs={{0,16},{8,24},{16,0},{24,8},{1,17},{9,25},{17,1},{25,9},{2,18},{10... | collective-permute-start | bytes 1966088 | tf_op jit(solution)/shard_map/ppermute | solution.py:863
  521.6 36.5 %collective-permute-start.50 = (bf16[160,2048]{1,0:T(8,128)(2,1)}, bf16[160,2048]{1,0:T(8,128)(2,1)}, u32[]{:S(2)}, u32[]{:S(2)}) collective-permute-start(bf16[160,2048]{1,0:T(8,128)(2,1)} %get-tuple-element.128.refs_2_), channel_id=1, source_target_pairs={{0,8},{8,0},{16,24},{24,16},{1,9},{9,1},{17,25},{25,17},{2,10},{10... | collective-permute-start | bytes 1966088 | tf_op jit(solution)/shard_map/ppermute | solution.py:863
  (103 other events, 1436.5 us)
Sparse Core Ops, SparseCore 0:
  11.0 34.3 all-gather.7
  47.6 28.5 all-gather.9
  79.7 32.5 all-gather.17
  114.4 59.1 all-gather.11
  175.0 59.0 all-gather.13
  235.6 59.0 all-gather.15
  297.7 62.7 reduce-scatter.5
  363.4 63.5 reduce-scatter.9
  429.8 63.2 reduce-scatter.7
  514.1 35.9 reduce-scatter.11
  575.4 52.1 reduce-scatter.13

commit v2 on v1

--- a/solution.py
+++ b/solution.py
@@ -53,6 +53,7 @@
     "down_product": 4,
     "output_gradient": 2,
     "project_back": 50,
+    "join_gradients": 50,
     "sum_output": 100,
     "sum_tokens": 100,
     "spread_up": 300,
@@ -735,14 +736,14 @@
     )
 
 
-def project_back(dq, d_kv, cos_t, sin_t, weight, rows, hat, before):
-    depth, wide = weight.shape
+def join_gradients(dq, d_kv, cos_t, sin_t, rows, hat, before):
+    depth, wide = hat.shape[1], dq.shape[1] + 128
     block = depth // 4
     first = before.shape[1]
 
-    def body(ins, outs, scratch):
-        dq_ref, kv_ref, cos_ref, sin_ref, w_ref, hat_ref, before_ref = ins
-        joined = scratch[0]
+    def body(ins, outs, _):
+        dq_ref, kv_ref, cos_ref, sin_ref, hat_ref, before_ref = ins
+        both, joined = outs
 
         @pl.when(pl.program_id(0) == 0)
         def _():
@@ -752,27 +753,40 @@
             turned = turn(values, cos_ref[...], -sin_ref[...])
             joined[:, wide - 128 :] = jnp.where(lane < 64, turned, values).astype(BF)
 
-        outs[0][:, :first] = before_ref[...]
-        outs[0][:, first:] = dot(hat_ref[...], joined[...], TN).astype(BF)
-        left = outs[1:]
+        both[:, :first] = before_ref[...]
+        both[:, first:] = dot(hat_ref[...], joined[...], TN).astype(BF)
+
+    return run(
+        body,
+        "join_gradients",
+        (4,),
+        [(v, whole(v.shape)) for v in (dq, d_kv, cos_t, sin_t)]
+        + [(hat, along_cols(4 * rows, block)), (before, down_rows(block, first))],
+        [
+            (array((depth, first + wide)), down_rows(block, first + wide)),
+            (array((4 * rows, wide)), whole((4 * rows, wide))),
+        ],
+    )
+
+
+def project_back(joined, weight, rows, needs):
+    depth, wide = weight.shape
+    block = depth // 4
+
+    def body(ins, outs, _):
+        left = outs
         for k in range(4):
             left = put_chunk(
-                left, dot(joined[k * rows : (k + 1) * rows, :], w_ref[...], NT)
+                left, dot(ins[0][k * rows : (k + 1) * rows, :], ins[1][...], NT)
             )
 
     return run(
         body,
         "project_back",
         (4,),
-        [(v, whole(v.shape)) for v in (dq, d_kv, cos_t, sin_t)]
-        + [
-            (weight, down_rows(block, wide)),
-            (hat, along_cols(4 * rows, block)),
-            (before, down_rows(block, first)),
-        ],
-        [(array((depth, first + wide)), down_rows(block, first + wide))]
-        + chunk_outs(range(4), rows, depth, block),
-        scratch=[pltpu.VMEM((4 * rows, wide), BF)],
+        [(joined, whole(joined.shape)), (weight, down_rows(block, wide))],
+        chunk_outs(range(4), rows, depth, block),
+        needs,
     )
 
 
@@ -1082,9 +1096,8 @@
     own_dkv = tie(own_dkv, out_raw, *terms[1:], downs_far)
     gate_part = tie(gate_part, own_dkv)
     gates_one, gates_two = hop(gate_part, 1), hop(gate_part, 2)
-    both_raw, *fs = project_back(
-        dq, own_dkv, cos_t, sin_t, w_qkv, rows, hat, out_raw
-    )
+    both_raw, d_qkv = join_gradients(dq, own_dkv, cos_t, sin_t, rows, hat, out_raw)
+    fs = list(project_back(d_qkv, w_qkv, rows, (both_raw,)))
     fs[5], fs[6] = (tie(f, gates_one, gates_two) for f in fs[5:])
     both_part = far(both_raw)
     layer_output = sum_output(terms, middle, (fs[6],))

time: 684 us -> 682 us (level)
  the two profiles are of different devices: /device:TPU:17 before, /device:TPU:28 now
where the time goes in v2:
time: 682 us; the launch traced here: 670 us
  Pallas kernels  314 us (46%)
  waiting for transfers between devices  185 us (27%)
  starting transfers between devices  69.6 us (10%)
  local copies, waits for them, and re-layouts  67.2 us (10%)
  other arithmetic  20 us (3%)
  between operations  15 us (2%)
    pallas_call x27, Pallas kernels, run(): pl.pallas_call(kernel, grid=grid, out_shape=tuple((shape for shape, _ in...  224 us
    ppermute x64, waiting for transfers between devices, hop(): return lax.ppermute(value, 'dp', [(i, i ^ step) for i in range(4)])  175 us
    ppermute x64, starting transfers between devices, hop(): return lax.ppermute(value, 'dp', [(i, i ^ step) for i in range(4)])  69 us
    pallas_call x1, Pallas kernels, attend_back(): pl.pallas_call(functools.partial(attend_back_kernel, rows=rows), grid_spe...  42.7 us
    unnamed x130, local copies, waits for them, and re-layouts  41 us
    pallas_call x1, Pallas kernels, attend(): pl.pallas_call(functools.partial(attend_kernel, rows=rows), grid_spec=plt...  29.3 us
  transfers between devices with their start and end apart: 78, of which 24 were waited for; matrix products, arithmetic and copies ran while one was open for 9% of the time, Pallas kernels for 46%

profile of v2, /device:TPU:28, one launch (start us, length us, event | category | flops | bytes accessed | tf_op | source)
XLA Modules:
  0.0 670.4 jit_solution(4871683559500155414)
XLA Ops:
  18.2 24.9 %collective-permute-done.1 = s32[1,2]{1,0:T(1,128)S(1)} collective-permute-done((s32[1,2]{1,0:T(1,128)}, s32[1,2]{1,0:T(1,128)S(1)}, u32[]{:S(2)}, u32[]{:S(2)}) %collective-permute-start.1) | collective-permute-done | bytes 40 | tf_op jit(solution)/shard_map/ppermute | solution.py:877
  87.1 23.2 %collective-permute-done.8.rest_1_.refs_2_.refs_9_.refs_12_ = bf16[1024,512]{1,0:T(8,128)(2,1)S(1)} collective-permute-done((bf16[1024,512]{1,0:T(8,128)(2,1)}, bf16[1024,512]{1,0:T(8,128)(2,1)S(1)}, u32[]{:S(2)}, u32[]{:S(2)}) %collective-permute-start.8) | collective-permute-done | bytes 1048608 | tf_op jit(solution)/shard_map/ppermute | solution.py:877
  123.4 29.3 %attend.1 = (bf16[1280,512]{1,0:T(8,128)(2,1)}, f32[4,1,2560]{2,1,0:T(1,128)}) custom-call(s32[9]{0:T(128)} %pad_add_fusion.3.where, bf16[1280,512]{1,0:T(8,128)(2,1)} %get-tuple-element.92.q_ref, bf16[8,1280,128]{2,1,0:T(8,128)(2,1)} %bitcast.23, s32[4,2,2560]{2,1,0:T(2,128)} %concatenate.38.bound_ref, bf16[1024,512]{1,0:T(8,128)(2,1)} %copy-done.8, ...), custom_call_target="tpu_custom_call" | custom-call | flops 320000000000 | bytes 1000000000 | tf_op jit(solution)/shard_map/attend/pallas_call | solution.py:327
  152.7 6.4 collective-permute-done.11.refs_1_.refs_0_
  173.0 6.4 collective-permute-done.16.refs_3_
  182.2 10.3 %output_product.1 = (bf16[160,2048]{1,0:T(8,128)(2,1)}, bf16[160,2048]{1,0:T(8,128)(2,1)}, f32[320,2048]{1,0:T(8,128)}, bf16[160,2048]{1,0:T(8,128)(2,1)}, bf16[160,2048]{1,0:T(8,128)(2,1)}) custom-call(s32[3]{0:T(128)} %pad_add_fusion.2.refs_0_, bf16[320,512]{1,0:T(8,128)(2,1)} %get-tuple-element.166.refs_1_, bf16[320,512]{1,0:T(8,128)(2,1)} %copy-done.18, ...), custom_call_target="tpu_custom_call" | custom-call | flops 2400000000 | bytes 7500000 | tf_op jit(solution)/shard_map/output_product/pallas_call | solution.py:98
  209.5 13.0 %hidden_back.1.refs_1_.refs_9_.refs_3_ = bf16[1280,1408]{1,0:T(8,128)(2,1)} custom-call(bf16[1280,2048]{1,0:T(8,128)(2,1)} %constant_dynamic-update-slice_fusion.refs_0_.refs_1_, bf16[1408,2048]{1,0:T(8,128)(2,1)} %all-gather.12.cloned.1.call-done.refs_1_, bf16[160,2048]{1,0:T(8,128)(2,1)} %get-tuple-element.96.refs_2_.refs_1_), custom_call_target="tpu_custom_call" | custom-call | flops 3200000000 | bytes 10000000 | tf_op jit(solution)/shard_map/hidden_back/pallas_call | solution.py:98
  230.2 12.5 %collective-permute-done.26.refs_7_.refs_2_ = bf16[160,2048]{1,0:T(8,128)(2,1)S(1)} collective-permute-done((bf16[160,2048]{1,0:T(8,128)(2,1)}, bf16[160,2048]{1,0:T(8,128)(2,1)S(1)}, u32[]{:S(2)}, u32[]{:S(2)}) %collective-permute-start.26) | collective-permute-done | bytes 655392 | tf_op jit(solution)/shard_map/ppermute | solution.py:877
  249.9 15.8 %gate_product.1 = (bf16[1280,1408]{1,0:T(8,128)(2,1)}, bf16[1280,1408]{1,0:T(8,128)(2,1)}, bf16[1280,2048]{1,0:T(8,128)(2,1)}) custom-call(bf16[160,2048]{1,0:T(8,128)(2,1)} %get-tuple-element.95.refs_1_.refs_0_, bf16[160,2048]{1,0:T(8,128)(2,1)} %get-tuple-element.96.refs_2_.refs_1_, bf16[160,2048]{1,0:T(8,128)(2,1)} %copy-done.10, ...), custom_call_target="tpu_custom_call" | custom-call | flops 1600000000 | bytes 5000000 | tf_op jit(solution)/shard_map/gate_product/pallas_call | solution.py:98
  265.7 12.9 %up_gradient.1.refs_4_ = bf16[2048,1408]{1,0:T(8,128)(2,1)} custom-call(bf16[1280,2048]{1,0:T(8,128)(2,1)} %get-tuple-element.98.refs_0_, bf16[1280,1408]{1,0:T(8,128)(2,1)} %get-tuple-element.101.refs_1_.refs_2_.refs_3_), custom_call_target="tpu_custom_call" | custom-call | flops 1600000000 | bytes 5000000 | tf_op jit(solution)/shard_map/up_gradient/pallas_call | solution.py:98
  283.6 9.6 %all-gather.16.cloned.1.call-done.refs_1_.refs_3_.refs_5_ = bf16[2048,1408]{1,0:T(8,128)(2,1)} async-done(((bf16[256,1408]{1,0:T(8,128)(2,1)}), bf16[2048,1408]{1,0:T(8,128)(2,1)}) %all-gather.16.cloned.1.call-update) | async-done | bytes 5767184 | tf_op jit(solution)/shard_map/all_gather | solution.py:976
  293.2 7.0 %up_product.2 = (bf16[1280,1408]{1,0:T(8,128)(2,1)}, bf16[1280,1408]{1,0:T(8,128)(2,1)}) custom-call(bf16[1280,2048]{1,0:T(8,128)(2,1)} %get-tuple-element.98.refs_0_, bf16[2048,1408]{1,0:T(8,128)(2,1)} %all-gather.16.cloned.1.call-done.refs_1_.refs_3_.refs_5_, bf16[1280,1408]{1,0:T(8,128)(2,1)} %get-tuple-element.100.refs_2_, ...), custom_call_target="tpu_custom_call" | custom-call | flops 80000000000 | bytes 250000000 | tf_op jit(solution)/shard_map/up_product/pallas_call | solution.py:98
  308.3 8.9 %back_first.1 = (bf16[160,2048]{1,0:T(8,128)(2,1)}, bf16[160,2048]{1,0:T(8,128)(2,1)}) custom-call(bf16[1280,1408]{1,0:T(8,128)(2,1)} %get-tuple-element.105.refs_0_.refs_5_, bf16[1280,1408]{1,0:T(8,128)(2,1)} %get-tuple-element.101.refs_1_.refs_2_.refs_3_, bf16[2048,1408]{1,0:T(8,128)(2,1)} %all-gather.14.cloned.1.call-done.refs_8_.refs_2_.refs_4_, ...), custom_call_target="tpu_custom_call" | custom-call | flops 3200000000 | bytes 10000000 | tf_op jit(solution)/shard_map/back_first/pallas_call | solution.py:98
  319.2 12.4 %up_product.3 = (bf16[1280,1408]{1,0:T(8,128)(2,1)}, bf16[1280,1408]{1,0:T(8,128)(2,1)}) custom-call(bf16[1280,2048]{1,0:T(8,128)(2,1)} %get-tuple-element.98.refs_0_, bf16[2048,1408]{1,0:T(8,128)(2,1)} %all-gather.16.cloned.1.call-done.refs_1_.refs_3_.refs_5_, ...), custom_call_target="tpu_custom_call", output_to_operand_aliasing={{0}: (4, {}), {1}: (5, {})} | custom-call | flops 80000000000 | bytes 250000000 | tf_op jit(solution)/shard_map/up_product/pallas_call | solution.py:98
  331.6 11.9 %down_gradient.1.refs_6_ = bf16[1408,2048]{1,0:T(8,128)(2,1)} custom-call(bf16[1280,1408]{1,0:T(8,128)(2,1)} %get-tuple-element.107.refs_0_, bf16[1280,2048]{1,0:T(8,128)(2,1)} %constant_dynamic-update-slice_fusion.refs_0_.refs_1_), custom_call_target="tpu_custom_call" | custom-call | flops 160000000 | bytes 500000 | tf_op jit(solution)/shard_map/down_gradient/pallas_call | solution.py:98
  344.7 12.8 %back_product.2 = (bf16[160,2048]{1,0:T(8,128)(2,1)}, bf16[160,2048]{1,0:T(8,128)(2,1)}, bf16[160,2048]{1,0:T(8,128)(2,1)}, bf16[160,2048]{1,0:T(8,128)(2,1)}) custom-call(bf16[1280,1408]{1,0:T(8,128)(2,1)} %get-tuple-element.108.refs_0_.refs_1_, bf16[1280,1408]{1,0:T(8,128)(2,1)} %get-tuple-element.108.refs_0_.refs_1_, ...), custom_call_target="tpu_custom_call" | custom-call | flops 3200000000 | bytes 10000000 | tf_op jit(solution)/shard_map/back_product/pallas_call | solution.py:98
  366.5 8.8 %back_product.3.refs_1_ = bf16[320,2048]{1,0:T(8,128)(2,1)} custom-call(bf16[1280,1408]{1,0:T(8,128)(2,1)} %get-tuple-element.108.refs_0_.refs_1_, bf16[1280,1408]{1,0:T(8,128)(2,1)} %get-tuple-element.101.refs_1_.refs_2_.refs_3_, bf16[2048,1408]{1,0:T(8,128)(2,1)} %all-gather.14.cloned.1.call-done.refs_8_.refs_2_.refs_4_, ...), custom_call_target="tpu_custom_call" | custom-call | flops 3200000000 | bytes 10000000 | tf_op jit(solution)/shard_map/back_product/pallas_call | solution.py:98
  380.0 12.4 %collective-permute-done.35.refs_2_ = bf16[160,2048]{1,0:T(8,128)(2,1)S(1)} collective-permute-done((bf16[160,2048]{1,0:T(8,128)(2,1)S(1)}, bf16[160,2048]{1,0:T(8,128)(2,1)S(1)}, u32[]{:S(2)}, u32[]{:S(2)}) %collective-permute-start.35) | collective-permute-done | bytes 655392 | tf_op jit(solution)/shard_map/ppermute | solution.py:877
  393.2 12.1 %middle_back.1 = (f32[320,2048]{1,0:T(8,128)}, bf16[320,1024]{1,0:T(8,128)(2,1)}, bf16[320,1024]{1,0:T(8,128)(2,1)}, bf16[320,1024]{1,0:T(8,128)(2,1)}, bf16[320,1024]{1,0:T(8,128)(2,1)}) custom-call(s32[3]{0:T(128)} %pad_add_fusion.2.refs_0_, bf16[320,2048]{1,0:T(8,128)(2,1)} %back_product.3.refs_1_, bf16[160,2048]{1,0:T(8,128)(2,1)} %copy-done.50, ...), custom_call_target="tpu_custom_call" | custom-call | flops 160000000000 | bytes 500000000 | tf_op jit(solution)/shard_map/middle_back/pallas_call | solution.py:98
  409.7 12.6 %gate_gradient.1.refs_2_ = bf16[2048,1408]{1,0:T(8,128)(2,1)} custom-call(bf16[1280,2048]{1,0:T(8,128)(2,1)} %get-tuple-element.98.refs_0_, bf16[1280,1408]{1,0:T(8,128)(2,1)} %get-tuple-element.108.refs_0_.refs_1_, bf16[320,1024]{1,0:T(8,128)(2,1)} %get-tuple-element.117.refs_2_), custom_call_target="tpu_custom_call" | custom-call | flops 1600000000 | bytes 5000000 | tf_op jit(solution)/shard_map/gate_gradient/pallas_call | solution.py:98
  422.4 12.4 %down_product.1 = (bf16[320,2048]{1,0:T(8,128)(2,1)}, bf16[160,2048]{1,0:T(8,128)(2,1)}, bf16[160,2048]{1,0:T(8,128)(2,1)}, bf16[160,2048]{1,0:T(8,128)(2,1)}, b...) custom-call(bf16[1280,1408]{1,0:T(8,128)(2,1)} %get-tuple-element.107.refs_0_, ...), custom_call_target="tpu_custom_call" | custom-call | flops 3200000000 | bytes 10000000 | tf_op jit(solution)/shard_map/down_product/pallas_call | solution.py:98
  443.1 10.2 %collective-permute-done.43.rest_2_ = bf16[256,1408]{1,0:T(8,128)(2,1)} collective-permute-done((bf16[256,1408]{1,0:T(8,128)(2,1)}, bf16[256,1408]{1,0:T(8,128)(2,1)}, u32[]{:S(2)}, u32[]{:S(2)}) %collective-permute-start.43) | collective-permute-done | bytes 720928 | tf_op jit(solution)/shard_map/ppermute | solution.py:877
  455.3 42.7 %attend_back.1 = (bf16[1280,512]{1,0:T(8,128)(2,1)}, bf16[8,1280,128]{2,1,0:T(8,128)(2,1)}) custom-call(s32[9]{0:T(128)} %pad_add_fusion.3.where, bf16[1280,512]{1,0:T(8,128)(2,1)} %get-tuple-element.92.q_ref, bf16[8,1280,128]{2,1,0:T(8,128)(2,1)} %bitcast.24, s32[4,2,2560]{2,1,0:T(2,128)} %concatenate.38.bound_ref, bf16[1280,1024]{1,0:T(8,128)(2,1)} %copy-done.15, ...), custom_call_target="tpu_custom_call" | custom-call | flops 799999983616 | bytes 2500000000 | tf_op jit(solution)/shard_map/attend_back/pallas_call | solution.py:433
  508.5 7.0 %output_gradient.1.refs_1_.refs_5_ = bf16[2048,512]{1,0:T(8,128)(2,1)} custom-call(bf16[1280,2048]{1,0:T(8,128)(2,1)} %constant_dynamic-update-slice_fusion.5.refs_17_.refs_0_, bf16[1280,1024]{1,0:T(8,128)(2,1)} %copy-done.15, bf16[160,2048]{1,0:T(8,128)(2,1)} %get-tuple-element.129.refs_2_), custom_call_target="tpu_custom_call" | custom-call | flops 1600000000 | bytes 5000000 | tf_op jit(solution)/shard_map/output_gradient/pallas_call | solution.py:98
  516.5 29.5 %collective-permute-done.51.refs_4_.refs_3_ = bf16[160,2048]{1,0:T(8,128)(2,1)S(1)} collective-permute-done((bf16[160,2048]{1,0:T(8,128)(2,1)}, bf16[160,2048]{1,0:T(8,128)(2,1)S(1)}, u32[]{:S(2)}, u32[]{:S(2)}) %collective-permute-start.51) | collective-permute-done | bytes 655392 | tf_op jit(solution)/shard_map/ppermute | solution.py:877
  551.1 9.5 %join_gradients.1 = (bf16[2048,1152]{1,0:T(8,128)(2,1)}, bf16[1280,640]{1,0:T(8,128)(2,1)}) custom-call(bf16[1280,512]{1,0:T(8,128)(2,1)} %get-tuple-element.132.refs_0_, bf16[1280,128]{1,0:T(8,128)(2,1)} %tie.41.refs_1_, f32[1280,128]{1,0:T(8,128)} %get-tuple-element.172.refs_2_.refs_3_.cos_ref, f32[1280,128]{1,0:T(8,128)} %get-tuple-element.173.refs_3_.refs_4_.sin_ref, ...), custom_call_target="tpu_custom_call" | custom-call | flops 40000000000 | bytes 125000000 | tf_op jit(solution)/shard_map/join_gradients/pallas_call | solution.py:98
  560.6 7.4 %project_back.1 = (bf16[320,2048]{1,0:T(8,128)(2,1)}, bf16[160,2048]{1,0:T(8,128)(2,1)}, bf16[160,2048]{1,0:T(8,128)(2,1)}, bf16[160,2048]{1,0:T(8,128)(2,1)}, b...) custom-call(bf16[1280,640]{1,0:T(8,128)(2,1)} %get-tuple-element.134.refs_0_, ...), custom_call_target="tpu_custom_call" | custom-call | flops 40000000000 | bytes 125000000 | tf_op jit(solution)/shard_map/project_back/pallas_call | solution.py:98
  576.3 6.8 %spread_up.1 = (f32[256,5632]{1,0:T(8,128)}, f32[256,1]{1,0:T(8,128)}) custom-call(s32[1]{0:T(128)} %bitcast.which.refs_0_, bf16[4,256,1408]{2,1,0:T(8,128)(2,1)} %pad_maximum_fusion.1.grads, f32[256,1]{1,0:T(8,128)} %copy.69.gain, bf16[256,5632]{1,0:T(8,128)(2,1)} %weight.3), custom_call_target="tpu_custom_call" | custom-call | flops 240000008192 | bytes 750000000 | tf_op jit(solution)/shard_map/spread_up/pallas_call | solution.py:175
  587.8 12.1 %collective-permute-done.58.refs_3_ = bf16[160,2048]{1,0:T(8,128)(2,1)} collective-permute-done((bf16[160,2048]{1,0:T(8,128)(2,1)}, bf16[160,2048]{1,0:T(8,128)(2,1)}, u32[]{:S(2)}, u32[]{:S(2)}) %collective-permute-start.58) | collective-permute-done | bytes 655392 | tf_op jit(solution)/shard_map/ppermute | solution.py:877
  619.2 6.8 %spread_gate.1 = (f32[256,5632]{1,0:T(8,128)}, f32[256,1]{1,0:T(8,128)}) custom-call(s32[1]{0:T(128)} %bitcast.which.refs_0_, bf16[4,256,1408]{2,1,0:T(8,128)(2,1)} %pad_maximum_fusion.grads, f32[256,1]{1,0:T(8,128)} %copy.69.gain, bf16[256,5632]{1,0:T(8,128)(2,1)} %weight.2), custom_call_target="tpu_custom_call" | custom-call | flops 80000000 | bytes 250000 | tf_op jit(solution)/shard_map/spread_gate/pallas_call | solution.py:175
  631.1 12.0 %collective-permute-done.61.refs_3_ = bf16[160,2048]{1,0:T(8,128)(2,1)} collective-permute-done((bf16[160,2048]{1,0:T(8,128)(2,1)}, bf16[160,2048]{1,0:T(8,128)(2,1)}, u32[]{:S(2)}, u32[]{:S(2)}) %collective-permute-start.61) | collective-permute-done | bytes 655392 | tf_op jit(solution)/shard_map/ppermute | solution.py:877
  643.1 6.5 sum_tokens.1
  (369 shorter events, 229.6 us)
Async XLA Ops:
  7.2 37.2 %all-gather.8.cloned.1.call-start = ((), (), s32[]{:S(2)}) async-start(), calls=%async_computation.5 | async-start | bytes 2949120 | tf_op jit(solution)/shard_map/all_gather | solution.py:976
  10.9 63.9 %all-gather.10.cloned.1.call-start = ((), (), s32[]{:S(2)}) async-start(), calls=%async_computation.6 | async-start | bytes 2359296 | tf_op jit(solution)/shard_map/all_gather | solution.py:976
  11.0 33.4 %collective-permute-start.5 = (bf16[320,2048]{1,0:T(8,128)(2,1)}, bf16[320,2048]{1,0:T(8,128)(2,1)}, u32[]{:S(2)}, u32[]{:S(2)}) collective-permute-start(bf16[320,2048]{1,0:T(8,128)(2,1)} %refs_5_.1), channel_id=1, source_target_pairs={{0,8},{8,0},{16,24},{24,16},{1,9},{9,1},{17,25},{25,17},{2,10},{10... | collective-permute-start | bytes 3932168 | tf_op jit(solution)/shard_map/ppermute | solution.py:877
  44.4 79.0 %all-gather.18.cloned.1.call-start = ((), (), s32[]{:S(2)}) async-start(), calls=%async_computation.15 | async-start | bytes 2949120 | tf_op jit(solution)/shard_map/all_gather | solution.py:1029
  77.9 131.6 %all-gather.12.cloned.1.call-start = ((), (), s32[]{:S(2)}) async-start(), calls=%async_computation.7 | async-start | bytes 6488064 | tf_op jit(solution)/shard_map/all_gather | solution.py:976
  78.9 171.0 %all-gather.14.cloned.1.call-start = ((), (), s32[]{:S(2)}) async-start(), calls=%async_computation.8 | async-start | bytes 6488064 | tf_op jit(solution)/shard_map/all_gather | solution.py:976
  84.8 208.4 %all-gather.16.cloned.1.call-start = ((), (), s32[]{:S(2)}) async-start(), calls=%async_computation.9 | async-start | bytes 6488064 | tf_op jit(solution)/shard_map/all_gather | solution.py:976
  110.8 281.5 %reduce-scatter.6.cloned.1.call-start = ((), (), s32[]{:S(2)}) async-start(), calls=%async_computation.10 | async-start | bytes 6488064 | tf_op jit(solution)/shard_map/reduce_scatter | solution.py:977
  115.6 43.5 %collective-permute-start.14 = (bf16[320,2048]{1,0:T(8,128)(2,1)}, bf16[320,2048]{1,0:T(8,128)(2,1)}, u32[]{:S(2)}, u32[]{:S(2)}) collective-permute-start(bf16[320,2048]{1,0:T(8,128)(2,1)} %tie.27.refs_0_), channel_id=1, source_target_pairs={{0,16},{8,24},{16,0},{24,8},{1,17},{9,25},{17,1},{25,9},{2,18},{10... | collective-permute-start | bytes 3932168 | tf_op jit(solution)/shard_map/ppermute | solution.py:877
  116.9 42.2 %collective-permute-start.13 = (bf16[320,2048]{1,0:T(8,128)(2,1)}, bf16[320,2048]{1,0:T(8,128)(2,1)}, u32[]{:S(2)}, u32[]{:S(2)}) collective-permute-start(bf16[320,2048]{1,0:T(8,128)(2,1)} %tie.27.refs_0_), channel_id=1, source_target_pairs={{0,8},{8,0},{16,24},{24,16},{1,9},{9,1},{17,25},{25,17},{2,10},{10... | collective-permute-start | bytes 3932168 | tf_op jit(solution)/shard_map/ppermute | solution.py:877
  120.1 39.0 %collective-permute-start.11 = (bf16[512,512]{1,0:T(8,128)(2,1)}, bf16[512,512]{1,0:T(8,128)(2,1)}, u32[]{:S(2)}, u32[]{:S(2)}) collective-permute-start(bf16[512,512]{1,0:T(8,128)(2,1)} %slice.60), channel_id=1, source_target_pairs={{0,8},{8,0},{16,24},{24,16},{1,9},{9,1},{17,25},{25,17},{2,10},{10... | collective-permute-start | bytes 1572872 | tf_op jit(solution)/shard_map/ppermute | solution.py:877
  122.7 36.3 %collective-permute-start.12 = (bf16[512,512]{1,0:T(8,128)(2,1)}, bf16[512,512]{1,0:T(8,128)(2,1)}, u32[]{:S(2)}, u32[]{:S(2)}) collective-permute-start(bf16[512,512]{1,0:T(8,128)(2,1)} %slice.61), channel_id=1, source_target_pairs={{0,16},{8,24},{16,0},{24,8},{1,17},{9,25},{17,1},{25,9},{2,18},{10... | collective-permute-start | bytes 1572872 | tf_op jit(solution)/shard_map/ppermute | solution.py:877
  193.7 34.9 %collective-permute-start.24 = (bf16[160,2048]{1,0:T(8,128)(2,1)S(1)}, bf16[160,2048]{1,0:T(8,128)(2,1)S(1)}, u32[]{:S(2)}, u32[]{:S(2)}) collective-permute-start(bf16[160,2048]{1,0:T(8,128)(2,1)S(1)} %copy-done.30), channel_id=1, source_target_pairs={{0,16},{8,24},{16,0},{24,8},{1,17},{9,25},{17,1},{25,9},{2,18},{10... | collective-permute-start | bytes 1966088 | tf_op jit(solution)/shard_map/ppermute | solution.py:877
  245.9 35.7 %collective-permute-start.29 = (bf16[160,2048]{1,0:T(8,128)(2,1)}, bf16[160,2048]{1,0:T(8,128)(2,1)S(1)}, u32[]{:S(2)}, u32[]{:S(2)}) collective-permute-start(bf16[160,2048]{1,0:T(8,128)(2,1)} %tie.35), channel_id=1, source_target_pairs={{0,16},{8,24},{16,0},{24,8},{1,17},{9,25},{17,1},{25,9},{2,18},{10... | collective-permute-start | bytes 1966088 | tf_op jit(solution)/shard_map/ppermute | solution.py:877
  246.2 47.0 %collective-permute-start.27 = (bf16[160,2048]{1,0:T(8,128)(2,1)}, bf16[160,2048]{1,0:T(8,128)(2,1)}, u32[]{:S(2)}, u32[]{:S(2)}) collective-permute-start(bf16[160,2048]{1,0:T(8,128)(2,1)} %tie.35), channel_id=1, source_target_pairs={{0,8},{8,0},{16,24},{24,16},{1,9},{9,1},{17,25},{25,17},{2,10},{10... | collective-permute-start | bytes 1966088 | tf_op jit(solution)/shard_map/ppermute | solution.py:877
  247.9 45.3 %collective-permute-start.30 = (bf16[160,2048]{1,0:T(8,128)(2,1)}, bf16[160,2048]{1,0:T(8,128)(2,1)}, u32[]{:S(2)}, u32[]{:S(2)}) collective-permute-start(bf16[160,2048]{1,0:T(8,128)(2,1)} %tie.36), channel_id=1, source_target_pairs={{0,16},{8,24},{16,0},{24,8},{1,17},{9,25},{17,1},{25,9},{2,18},{10... | collective-permute-start | bytes 1966088 | tf_op jit(solution)/shard_map/ppermute | solution.py:877
  248.6 33.6 %collective-permute-start.28 = (bf16[160,2048]{1,0:T(8,128)(2,1)}, bf16[160,2048]{1,0:T(8,128)(2,1)}, u32[]{:S(2)}, u32[]{:S(2)}) collective-permute-start(bf16[160,2048]{1,0:T(8,128)(2,1)} %tie.36), channel_id=1, source_target_pairs={{0,8},{8,0},{16,24},{24,16},{1,9},{9,1},{17,25},{25,17},{2,10},{10... | collective-permute-start | bytes 1966088 | tf_op jit(solution)/shard_map/ppermute | solution.py:877
  278.7 174.6 %reduce-scatter.10.cloned.1.call-start = ((), (), s32[]{:S(2)}) async-start(), calls=%async_computation.12 | async-start | bytes 6488064 | tf_op jit(solution)/shard_map/reduce_scatter | solution.py:977
  343.6 154.5 %reduce-scatter.8.cloned.1.call-start = ((), (), s32[]{:S(2)}) async-start(), calls=%async_computation.11 | async-start | bytes 6488064 | tf_op jit(solution)/shard_map/reduce_scatter | solution.py:977
  406.2 34.1 %collective-permute-start.41 = (bf16[320,1024]{1,0:T(8,128)(2,1)}, bf16[320,1024]{1,0:T(8,128)(2,1)}, u32[]{:S(2)}, u32[]{:S(2)}) collective-permute-start(bf16[320,1024]{1,0:T(8,128)(2,1)} %get-tuple-element.122), channel_id=1, source_target_pairs={{0,24},{8,16},{16,8},{24,0},{1,25},{9,17},{17,9},{25,1},{2,26},{10... | collective-permute-start | bytes 1966088 | tf_op jit(solution)/shard_map/ppermute | solution.py:877
  408.8 44.6 %collective-permute-start.43 = (bf16[256,1408]{1,0:T(8,128)(2,1)}, bf16[256,1408]{1,0:T(8,128)(2,1)}, u32[]{:S(2)}, u32[]{:S(2)}) collective-permute-start(bf16[256,1408]{1,0:T(8,128)(2,1)} %reduce-scatter.6.cloned.1.call-done.refs_16_.refs_0_), channel_id=1, source_target_pairs={{0,16},{8,24},{16,0},{24,8},{1,17},{9,25},{17,1},{25,9},{2,18},{10... | collective-permute-start | bytes 2162696 | tf_op jit(solution)/shard_map/ppermute | solution.py:877
  409.3 44.4 %collective-permute-start.42 = (bf16[256,1408]{1,0:T(8,128)(2,1)}, bf16[256,1408]{1,0:T(8,128)(2,1)}, u32[]{:S(2)}, u32[]{:S(2)}) collective-permute-start(bf16[256,1408]{1,0:T(8,128)(2,1)} %reduce-scatter.6.cloned.1.call-done.refs_16_.refs_0_), channel_id=1, source_target_pairs={{0,8},{8,0},{16,24},{24,16},{1,9},{9,1},{17,25},{25,17},{2,10},{10... | collective-permute-start | bytes 2162696 | tf_op jit(solution)/shard_map/ppermute | solution.py:877
  422.3 123.7 %reduce-scatter.12.cloned.1.call-start = ((), (), s32[]{:S(2)}) async-start(), calls=%async_computation.13 | async-start | bytes 2949120 | tf_op jit(solution)/shard_map/reduce_scatter | solution.py:977
  434.7 63.3 %collective-permute-start.44 = (bf16[160,2048]{1,0:T(8,128)(2,1)}, bf16[160,2048]{1,0:T(8,128)(2,1)}, u32[]{:S(2)}, u32[]{:S(2)}) collective-permute-start(bf16[160,2048]{1,0:T(8,128)(2,1)} %get-tuple-element.126), channel_id=1, source_target_pairs={{0,8},{8,0},{16,24},{24,16},{1,9},{9,1},{17,25},{25,17},{2,10},{10... | collective-permute-start | bytes 1966088 | tf_op jit(solution)/shard_map/ppermute | solution.py:877
  437.9 60.2 %collective-permute-start.45 = (bf16[160,2048]{1,0:T(8,128)(2,1)}, bf16[160,2048]{1,0:T(8,128)(2,1)}, u32[]{:S(2)}, u32[]{:S(2)}) collective-permute-start(bf16[160,2048]{1,0:T(8,128)(2,1)} %get-tuple-element.124.rest_0_), channel_id=1, source_target_pairs={{0,16},{8,24},{16,0},{24,8},{1,17},{9,25},{17,1},{25,9},{2,18},{10... | collective-permute-start | bytes 1966088 | tf_op jit(solution)/shard_map/ppermute | solution.py:877
  440.3 57.7 %collective-permute-start.48 = (bf16[256,1408]{1,0:T(8,128)(2,1)}, bf16[256,1408]{1,0:T(8,128)(2,1)}, u32[]{:S(2)}, u32[]{:S(2)}) collective-permute-start(bf16[256,1408]{1,0:T(8,128)(2,1)} %reduce-scatter.6.cloned.1.call-done.refs_16_.refs_0_), channel_id=1, source_target_pairs={{0,24},{8,16},{16,8},{24,0},{1,25},{9,17},{17,9},{25,1},{2,26},{10... | collective-permute-start | bytes 2162696 | tf_op jit(solution)/shard_map/ppermute | solution.py:877
  453.3 44.8 %collective-permute-start.47 = (bf16[176,2048]{1,0:T(8,128)(2,1)}, bf16[176,2048]{1,0:T(8,128)(2,1)}, u32[]{:S(2)}, u32[]{:S(2)}) collective-permute-start(bf16[176,2048]{1,0:T(8,128)(2,1)} %reduce-scatter.10.cloned.1.call-done.refs_1_), channel_id=1, source_target_pairs={{0,16},{8,24},{16,0},{24,8},{1,17},{9,25},{17,1},{25,9},{2,18},{10... | collective-permute-start | bytes 2162696 | tf_op jit(solution)/shard_map/ppermute | solution.py:877
  453.7 44.4 %collective-permute-start.46 = (bf16[176,2048]{1,0:T(8,128)(2,1)}, bf16[176,2048]{1,0:T(8,128)(2,1)}, u32[]{:S(2)}, u32[]{:S(2)}) collective-permute-start(bf16[176,2048]{1,0:T(8,128)(2,1)} %reduce-scatter.10.cloned.1.call-done.refs_1_), channel_id=1, source_target_pairs={{0,8},{8,0},{16,24},{24,16},{1,9},{9,1},{17,25},{25,17},{2,10},{10... | collective-permute-start | bytes 2162696 | tf_op jit(solution)/shard_map/ppermute | solution.py:877
  498.2 129.5 %reduce-scatter.14.cloned.1.call-start = ((), (), s32[]{:S(2)}) async-start(), calls=%async_computation.14 | async-start | bytes 5308416 | tf_op jit(solution)/shard_map/reduce_scatter | solution.py:977
  502.2 43.8 %collective-permute-start.53 = (bf16[176,2048]{1,0:T(8,128)(2,1)S(1)}, bf16[176,2048]{1,0:T(8,128)(2,1)S(1)}, u32[]{:S(2)}, u32[]{:S(2)}) collective-permute-start(bf16[176,2048]{1,0:T(8,128)(2,1)S(1)} %copy-done.19), channel_id=1, source_target_pairs={{0,24},{8,16},{16,8},{24,0},{1,25},{9,17},{17,9},{25,1},{2,26},{10... | collective-permute-start | bytes 2162696 | tf_op jit(solution)/shard_map/ppermute | solution.py:877
  506.5 39.5 %collective-permute-start.51 = (bf16[160,2048]{1,0:T(8,128)(2,1)}, bf16[160,2048]{1,0:T(8,128)(2,1)S(1)}, u32[]{:S(2)}, u32[]{:S(2)}) collective-permute-start(bf16[160,2048]{1,0:T(8,128)(2,1)} %get-tuple-element.130), channel_id=1, source_target_pairs={{0,16},{8,24},{16,0},{24,8},{1,17},{9,25},{17,1},{25,9},{2,18},{10... | collective-permute-start | bytes 1966088 | tf_op jit(solution)/shard_map/ppermute | solution.py:877
  508.0 38.0 %collective-permute-start.50 = (bf16[160,2048]{1,0:T(8,128)(2,1)}, bf16[160,2048]{1,0:T(8,128)(2,1)}, u32[]{:S(2)}, u32[]{:S(2)}) collective-permute-start(bf16[160,2048]{1,0:T(8,128)(2,1)} %get-tuple-element.129.refs_2_), channel_id=1, source_target_pairs={{0,8},{8,0},{16,24},{24,16},{1,9},{9,1},{17,25},{25,17},{2,10},{10... | collective-permute-start | bytes 1966088 | tf_op jit(solution)/shard_map/ppermute | solution.py:877
  (103 other events, 1503.8 us)
Sparse Core Ops, SparseCore 0:
  11.0 32.8 all-gather.7
  46.1 28.5 all-gather.9
  78.0 32.7 all-gather.17
  112.9 59.0 all-gather.11
  173.4 59.0 all-gather.13
  234.1 59.0 all-gather.15
  296.1 63.3 reduce-scatter.5
  362.3 63.2 reduce-scatter.9
  428.5 63.2 reduce-scatter.7
  498.3 47.3 reduce-scatter.11
  560.7 53.0 reduce-scatter.13
